TPU v7x, 128 devices: a whole 4x4x4 slice. The times are simulated.
128 devices in a mesh: role: 2 (over core), batch: 8 (over y_lo, x), tensor: 8 (over z, y_hi).
Axes of the slice: x: 4, y: 4 (y_hi: 2, y_lo: 2; y = y_hi * 2 + y_lo), z: 4, core: 2. Of those that a mesh axis runs over, the one named last changes fastest.
Arguments:
- queries: bfloat16 [128, 8192], P(('role', 'batch'), 'tensor'), may hold values from -200 to 200
- new_keys: bfloat16 [128, 1024], P(('role', 'batch'), 'tensor'), may hold values from -6 to 6
- new_values: bfloat16 [128, 1024], P(('role', 'batch'), 'tensor'), may hold values from -6 to 6
- key_cache: bfloat16 [128, 8, 3072, 128], P(('role', 'batch'), 'tensor'), may hold values from -6 to 6
- value_cache: bfloat16 [128, 8, 3072, 128], P(('role', 'batch'), 'tensor'), may hold values from -6 to 6
- lengths: int32 [128], P(('role', 'batch')), may hold values from 1 to 3072, as said below
- residual: bfloat16 [128, 8192], P(('role', 'batch'), 'tensor'), may hold values from -6 to 6
- norm_gain: bfloat16 [8192], replicated, may hold values from 0.25 to 1.75
- gate_weight: bfloat16 [8192, 28672], P(None, ('role', 'batch', 'tensor')), may hold values from -0.0625 to 0.0625
- up_weight: bfloat16 [8192, 28672], P(None, ('role', 'batch', 'tensor')), may hold values from -0.0625 to 0.0625
- down_weight: bfloat16 [28672, 8192], P(('role', 'batch', 'tensor')), may hold values from -0.125 to 0.125
Outputs:
- layer_out: bfloat16 [128, 8192], P(('role', 'batch'), 'tensor')
Inputs may be any that keep to these rules, and one draw needn't show every extreme that they name: `lengths`: each row has 1 to 3072 cached tokens, and some row has exactly 3072.
All inputs are finite; a program needn't handle non-finite values.
Results may differ from a plain program's by a relative error of at most 0.0063.
Values may be sent and summed in bfloat16 or wider, within the bound.
No kernel may reach another device: no remote copies, remote signals or barrier semaphores. Data moves between devices by JAX's collectives and lax.ppermute only.
A program may use at most 128 MiB of HBM per device.

v0:
```python
import jax
import jax.numpy as jnp
from jax import lax
from jax.sharding import PartitionSpec as P


def local(
    queries,
    new_keys,
    new_values,
    key_cache,
    value_cache,
    lengths,
    residual,
    norm_gain,
    gate_weight,
    up_weight,
    down_weight,
):
    local_rows = queries.shape[0]
    head_size = new_keys.shape[1]
    group_heads = queries.shape[1] // head_size
    cache_len = key_cache.shape[2]
    factor = head_size ** (-0.5)
    query_heads = queries.reshape(local_rows, group_heads, head_size)
    cache_keys = key_cache.reshape(local_rows, cache_len, head_size)
    cache_values = value_cache.reshape(local_rows, cache_len, head_size)
    scores = (
        jnp.einsum("rqd,rtd->rqt", query_heads, cache_keys, preferred_element_type=jnp.float32)
        * factor
    )
    position = jnp.arange(cache_len)
    scores = jnp.where(position[None, None, :] < lengths[:, None, None], scores, -jnp.inf)
    own_score = (
        jnp.einsum("rqd,rd->rq", query_heads, new_keys, preferred_element_type=jnp.float32) * factor
    )
    top_score = jnp.maximum(jnp.max(scores, axis=-1), own_score)
    weights = jnp.exp(scores - top_score[..., None])
    own_weight = jnp.exp(own_score - top_score)
    denominator = jnp.sum(weights, axis=-1) + own_weight
    weights_low = (weights / denominator[..., None]).astype(jnp.bfloat16)
    own_low = (own_weight / denominator).astype(jnp.bfloat16)
    mixed = jnp.einsum(
        "rqt,rtd->rqd", weights_low, cache_values, preferred_element_type=jnp.float32
    )
    mixed = (
        mixed + own_low.astype(jnp.float32)[..., None] * new_values.astype(jnp.float32)[:, None, :]
    )
    attended = mixed.reshape(local_rows, group_heads * head_size)
    hidden_state = (residual.astype(jnp.float32) + attended).astype(jnp.bfloat16)
    full_rows = lax.all_gather(hidden_state, "tensor", axis=1, tiled=True)
    all_hidden = lax.all_gather(full_rows, ("role", "batch"), axis=0, tiled=True)
    wide = all_hidden.astype(jnp.float32)
    mean_square = jnp.mean(wide * wide, axis=-1, keepdims=True)
    normed = (wide * lax.rsqrt(mean_square + 1e-05) * norm_gain.astype(jnp.float32)).astype(
        jnp.bfloat16
    )
    gate = jnp.dot(normed, gate_weight, preferred_element_type=jnp.float32)
    up_part = jnp.dot(normed, up_weight, preferred_element_type=jnp.float32)
    activation = (jax.nn.silu(gate) * up_part).astype(jnp.bfloat16)
    partial_out = jnp.dot(activation, down_weight, preferred_element_type=jnp.float32)
    own_rows = lax.psum_scatter(partial_out, ("role", "batch"), scatter_dimension=0, tiled=True)
    summed = lax.psum_scatter(own_rows, "tensor", scatter_dimension=1, tiled=True)
    return (hidden_state.astype(jnp.float32) + summed).astype(jnp.bfloat16)


def solution(mesh):
    in_specs = (
        P(("role", "batch"), "tensor"),
        P(("role", "batch"), "tensor"),
        P(("role", "batch"), "tensor"),
        P(("role", "batch"), "tensor", None, None),
        P(("role", "batch"), "tensor", None, None),
        P(("role", "batch")),
        P(("role", "batch"), "tensor"),
        P(),
        P(None, ("role", "batch", "tensor")),
        P(None, ("role", "batch", "tensor")),
        P(("role", "batch", "tensor"), None),
    )
    out_specs = P(("role", "batch"), "tensor")
    return jax.shard_map(local, mesh=mesh, in_specs=in_specs, out_specs=out_specs, check_vma=False)
```

profile of v0, /device:TPU:0, one launch (start us, length us, event | category | flops | bytes accessed | tf_op | source)
XLA Modules:
  0.0 259.5 jit_solution(16675498872882781675)
XLA Ops:
  6.5 0.0 copy-start
  6.5 0.0 all-gather.2.cloned.1.call-start
  6.5 0.7 convert_element_type.40
  7.2 0.7 iota_compare_fusion
  8.0 0.0 copy-done
  8.0 0.8 fusion.35
  8.8 4.8 %fusion.42 = (f32[8,8]{1,0:T(8,128)S(1)}, f32[8,8,3072]{2,1,0:T(8,128)S(1)}) fusion(bf16[8,1,3072,128]{3,2,1,0:T(8,128)(2,1)} %param.14, bf16[8,8,128]{2,0,1:T(8,128)(2,1)} %bitcast.31, pred[8,3072]{1,0:T(8,128)(4,1)S(1)} %iota_compare_fusion), kind=kOutput, calls=%fused_computation.43 | convolution fusion | flops 50921408 | bytes 7119104 | tf_op jit(solution)/shard_map/rqd,rtd->rqt/dot_general | solution.py:29
  13.6 0.3 fusion.21
  13.9 0.0 copy-start.4
  13.9 0.0 copy-start.3
  13.9 1.0 fusion.18
  14.9 37.8 %all_gather.6 = bf16[8,8192]{1,0:T(8,128)(2,1)} all-gather(bf16[8,1024]{1,0:T(8,128)(2,1)S(1)} %fusion.34), channel_id=1, replica_groups=mesh['role'=2,'batch'=8,'tensor'=8] {'tensor'}, dimensions={1}, use_global_device_ids=true | all-gather | bytes 147456 | tf_op jit(solution)/shard_map/all_gather | solution.py:51
  52.7 0.0 all-gather.2.cloned.1.call-update
  52.7 0.0 reduce-scatter.3.cloned.1.call-start
  52.8 35.1 %all-gather.2.cloned.1.call-done = bf16[128,8192]{1,0:T(8,128)(2,1)} async-done(((bf16[8,8192]{1,0:T(8,128)(2,1)}), bf16[128,8192]{1,0:T(8,128)(2,1)}) %all-gather.2.cloned.1.call-update) | async-done | bytes 2097168 | tf_op jit(solution)/shard_map/all_gather | solution.py:52
  87.9 2.1 fusion.4
  90.0 4.0 %fusion.24 = f32[128,224]{0,1:T(8,128)S(1)} fusion(bf16[8192,224]{0,1:T(8,128)(2,1)} %param.19, bf16[128,8192]{1,0:T(8,128)(2,1)} %all-gather.2.cloned.1.call-done, f32[8192]{0:T(1024)S(1)} %convert_element_type.44, f32[128]{0:T(128)S(1)} %add_rsqrt_fusion), kind=kOutput, calls=%fused_computation.19 | convolution fusion | flops 473956352 | bytes 5915136 | tf_op jit(solution)/shard_map/dot_general | solution.py:58
  94.0 8.1 %fusion.14 = f32[128,8192]{1,0:T(8,128)} fusion(bf16[224,8192]{1,0:T(8,128)(2,1)} %param.21, bf16[8192,224]{0,1:T(8,128)(2,1)} %param.20, bf16[128,8192]{1,0:T(8,128)(2,1)S(1)} %copy-done.2, f32[8192]{0:T(1024)S(1)} %convert_element_type.44, f32[128]{0:T(128)S(1)} %add_rsqrt_fusion, f32[128,224]{0,1:T(8,128)S(1)} %fusion.24), kind=kOutput, calls=%fused_computation.13 | convolution fusion | flops 943890432 | bytes 13779456 | tf_op jit(solution)/shard_map/dot_general | solution.py:61
  102.1 0.0 reduce-scatter.3.cloned.1.call-update
  102.2 0.0 reduce-scatter.5.cloned.1.call-start
  102.2 73.3 %reduce-scatter.3.cloned.1.call-done = f32[8,8192]{1,0:T(8,128)} async-done(((f32[128,8192]{1,0:T(8,128)}), f32[8,8192]{1,0:T(8,128)}) %reduce-scatter.3.cloned.1.call-update) | async-done | bytes 262160 | tf_op jit(solution)/shard_map/reduce_scatter | solution.py:62
  175.5 0.0 reduce-scatter.5.cloned.1.call-update
  175.5 76.1 %reduce-scatter.5.cloned.1.call-done = f32[8,1024]{1,0:T(8,128)} async-done(((f32[8,8192]{1,0:T(8,128)}), f32[8,1024]{1,0:T(8,128)}) %reduce-scatter.5.cloned.1.call-update) | async-done | bytes 32784 | tf_op jit(solution)/shard_map/reduce_scatter | solution.py:63
  251.6 1.4 add_convert_fusion
  (11 shorter events, 0.1 us)
Async XLA Ops:
  6.5 1.4 copy-start
  6.5 81.4 %all-gather.2.cloned.1.call-start = ((), (), s32[]{:S(2)}) async-start(), calls=%async_computation.2 | async-start | bytes 2228224 | tf_op jit(solution)/shard_map/all_gather | solution.py:52
  8.8 5.1 %copy-start.1 = (bf16[8,1,3072,128]{3,2,1,0:T(8,128)(2,1)S(1)}, bf16[8,1,3072,128]{3,2,1,0:T(8,128)(2,1)}, u32[]{:S(2)}) copy-start(bf16[8,1,3072,128]{3,2,1,0:T(8,128)(2,1)} %param.15) | copy-start | bytes 18874372
  13.9 1.0 copy-start.4
  13.9 38.9 %copy-start.3 = (bf16[8192]{0:T(1024)(128)(2,1)S(1)}, bf16[8192]{0:T(1024)(128)(2,1)}, u32[]{:S(2)}) copy-start(bf16[8192]{0:T(1024)(128)(2,1)} %param.18) | copy-start | bytes 49156
  52.7 122.8 %reduce-scatter.3.cloned.1.call-start = ((), (), s32[]{:S(2)}) async-start(), calls=%async_computation.3 | async-start | bytes 4456448 | tf_op jit(solution)/shard_map/reduce_scatter | solution.py:62
  90.0 4.0 %copy-start.2 = (bf16[128,8192]{1,0:T(8,128)(2,1)S(1)}, bf16[128,8192]{1,0:T(8,128)(2,1)}, u32[]{:S(2)}) copy-start(bf16[128,8192]{1,0:T(8,128)(2,1)} %all-gather.2.cloned.1.call-done) | copy-start | bytes 6291460
  102.2 149.5 %reduce-scatter.5.cloned.1.call-start = ((), (), s32[]{:S(2)}) async-start(), calls=%async_computation.4 | async-start | bytes 294912 | tf_op jit(solution)/shard_map/reduce_scatter | solution.py:63
Sparse Core Ops, SparseCore 0:
  52.8 35.0 all-gather.1
  102.3 73.1 reduce-scatter.2
  179.0 72.5 reduce-scatter.4
where the time goes:
time: 260 us
  waiting for transfers between devices  185 us (71%)
  blocking collectives  37.8 us (15%)
  matrix products  18.7 us (7%)
  between operations  13.2 us (5%)
  other arithmetic  5.2 us (2%)
    reduce_scatter x1, waiting for transfers between devices, local(): lax.psum_scatter(own_rows, 'tensor', scatter_dimension=1, tiled=True)  76.1 us
    reduce_scatter x1, waiting for transfers between devices, local(): lax.psum_scatter(partial_out, ('role', 'batch'), scatter_dimension=0, til...  73.3 us
    all_gather x1, blocking collectives, local(): full_rows = lax.all_gather(hidden_state, 'tensor', axis=1, tiled=True)  37.8 us
    all_gather x1, waiting for transfers between devices, local(): lax.all_gather(full_rows, ('role', 'batch'), axis=0, tiled=True)  35.1 us
    dot_general x1, matrix products, local(): jnp.dot(activation, down_weight, preferred_element_type=jnp.float32)  8.1 us
  transfers between devices with their start and end apart: 3, of which 3 were waited for; matrix products, arithmetic and copies ran while one was open for 0% of the time, Pallas kernels for 0%

commit v1 on v0

v1 whole, which is shorter than its diff:
```python
import jax
import jax.numpy as jnp
from jax import lax
from jax.sharding import PartitionSpec as P

AXES = ("role", "batch", "tensor")
CHIPS = ("batch", "tensor")


def local(
    queries,
    new_keys,
    new_values,
    key_cache,
    value_cache,
    lengths,
    residual,
    norm_gain,
    gate_weight,
    up_weight,
    down_weight,
):
    local_rows = queries.shape[0]
    head_size = new_keys.shape[1]
    group_heads = queries.shape[1] // head_size
    cache_len = key_cache.shape[2]
    width = queries.shape[1]
    batch = lax.axis_size("batch")
    tensor = lax.axis_size("tensor")
    chips = batch * tensor
    swap = [(0, 1), (1, 0)]
    gates = (gate_weight, lax.ppermute(gate_weight, "role", swap))
    ups = (up_weight, lax.ppermute(up_weight, "role", swap))
    downs = (down_weight, lax.ppermute(down_weight, "role", swap))

    factor = head_size ** (-0.5)
    query_heads = queries.reshape(local_rows, group_heads, head_size)
    cache_keys = key_cache.reshape(local_rows, cache_len, head_size)
    cache_values = value_cache.reshape(local_rows, cache_len, head_size)
    scores = (
        jnp.einsum("rqd,rtd->rqt", query_heads, cache_keys, preferred_element_type=jnp.float32)
        * factor
    )
    position = jnp.arange(cache_len)
    scores = jnp.where(position[None, None, :] < lengths[:, None, None], scores, -jnp.inf)
    own_score = (
        jnp.einsum("rqd,rd->rq", query_heads, new_keys, preferred_element_type=jnp.float32) * factor
    )
    top_score = jnp.maximum(jnp.max(scores, axis=-1), own_score)
    weights = jnp.exp(scores - top_score[..., None])
    own_weight = jnp.exp(own_score - top_score)
    denominator = jnp.sum(weights, axis=-1) + own_weight
    weights_low = (weights / denominator[..., None]).astype(jnp.bfloat16)
    own_low = (own_weight / denominator).astype(jnp.bfloat16)
    mixed = jnp.einsum(
        "rqt,rtd->rqd", weights_low, cache_values, preferred_element_type=jnp.float32
    )
    mixed = (
        mixed + own_low.astype(jnp.float32)[..., None] * new_values.astype(jnp.float32)[:, None, :]
    )
    attended = mixed.reshape(local_rows, width)
    hidden_state = (residual.astype(jnp.float32) + attended).astype(jnp.bfloat16)

    copies = jnp.broadcast_to(hidden_state[None], (chips, local_rows, width))
    pieces = lax.all_to_all(copies, CHIPS, 0, 0, tiled=True)
    all_hidden = (
        pieces.reshape(batch, tensor, local_rows, width)
        .transpose(0, 2, 1, 3)
        .reshape(batch * local_rows, tensor * width)
    )
    wide = all_hidden.astype(jnp.float32)
    mean_square = jnp.mean(wide * wide, axis=-1, keepdims=True)
    normed = (wide * lax.rsqrt(mean_square + 1e-05) * norm_gain.astype(jnp.float32)).astype(
        jnp.bfloat16
    )
    partial_out = 0.0
    for gate_part, up_part, down_part in zip(gates, ups, downs):
        gate = jnp.dot(normed, gate_part, preferred_element_type=jnp.float32)
        up = jnp.dot(normed, up_part, preferred_element_type=jnp.float32)
        activation = (jax.nn.silu(gate) * up).astype(jnp.bfloat16)
        partial_out += jnp.dot(activation, down_part, preferred_element_type=jnp.float32)
    sent = (
        partial_out.astype(jnp.bfloat16)
        .reshape(batch, local_rows, tensor, width)
        .transpose(0, 2, 1, 3)
        .reshape(chips, local_rows, width)
    )
    received = lax.all_to_all(sent, CHIPS, 0, 0, tiled=True)
    summed = jnp.sum(received.astype(jnp.float32), axis=0)
    return (hidden_state.astype(jnp.float32) + summed).astype(jnp.bfloat16)


def solution(mesh):
    rows = ("role", "batch")
    in_specs = (
        P(rows, "tensor"),
        P(rows, "tensor"),
        P(rows, "tensor"),
        P(rows, "tensor", None, None),
        P(rows, "tensor", None, None),
        P(rows),
        P(rows, "tensor"),
        P(),
        P(None, AXES),
        P(None, AXES),
        P(AXES, None),
    )
    return jax.shard_map(
        local, mesh=mesh, in_specs=in_specs, out_specs=P(rows, "tensor"), check_vma=False
    )
```

time: 260 us -> 83.2 us (0.32)
  waiting for transfers between devices: 185 us -> 17.9 us
  blocking collectives: 37.8 us -> 22.6 us
  between operations: 13.2 us -> 0.12 us
  starting transfers between devices: 0.09 us -> 12.2 us
  matrix products: 18.7 us -> 24 us
  local copies, waits for them, and re-layouts: 0.02 us -> 2.7 us
    reduce_scatter x2 -> x0, waiting for transfers between devices: 149 us -> none  [the longest x1 76.1 us: local(): lax.psum_scatter(own_rows, 'tensor', scatter_dimension=1, tiled=True)]
    all_gather x1 -> x0, blocking collectives: 37.8 us -> none  [local(): full_rows = lax.all_gather(hidden_state, 'tensor', axis=1, tiled=True)]
    all_gather x1 -> x0, waiting for transfers between devices: 35.1 us -> none  [local(): lax.all_gather(full_rows, ('role', 'batch'), axis=0, tiled=True)]
    all_to_all x0 -> x1, blocking collectives: none -> 22.6 us  [local(): received = lax.all_to_all(sent, CHIPS, 0, 0, tiled=True)]
    all_to_all x0 -> x1, waiting for transfers between devices: none -> 17.9 us  [local(): pieces = lax.all_to_all(copies, CHIPS, 0, 0, tiled=True)]
    all_to_all x0 -> x1, starting transfers between devices: none -> 11.5 us  [local(): pieces = lax.all_to_all(copies, CHIPS, 0, 0, tiled=True)]
    dot_general x2 -> x4, matrix products: 12.1 us -> 17.4 us  [the longest x2 12.8 us: local(): jnp.dot(activation, down_part, preferred_element_type=jnp.float32)]
  transfers between devices with their start and end apart: 3 -> 4, of which waited for: 3 -> 1; matrix products, arithmetic and copies ran while one was open for 0% -> 14% of each run, Pallas kernels for 0% -> 0%
where the time goes in v1:
time: 83.2 us; the launch traced here: 82.8 us
  matrix products  24 us (29%)
  blocking collectives  22.6 us (27%)
  waiting for transfers between devices  17.9 us (22%)
  starting transfers between devices  12.2 us (15%)
  other arithmetic  3.37 us (4%)
  local copies, waits for them, and re-layouts  2.7 us (3%)
    all_to_all x1, blocking collectives, local(): received = lax.all_to_all(sent, CHIPS, 0, 0, tiled=True)  22.6 us
    all_to_all x1, waiting for transfers between devices, local(): pieces = lax.all_to_all(copies, CHIPS, 0, 0, tiled=True)  17.9 us
    dot_general x2, matrix products, local(): jnp.dot(activation, down_part, preferred_element_type=jnp.float32)  12.8 us
    all_to_all x1, starting transfers between devices, local(): pieces = lax.all_to_all(copies, CHIPS, 0, 0, tiled=True)  11.5 us
    dot_general x1, matrix products, local(): jnp.einsum('rqd,rtd->rqt', query_heads, cache_keys, preferred_element_typ...  4.76 us
    dot_general x2, matrix products, local(): gate = jnp.dot(normed, gate_part, preferred_element_type=jnp.float32)  4.56 us
  transfers between devices with their start and end apart: 4, of which 1 were waited for; matrix products, arithmetic and copies ran while one was open for 14% of the time, Pallas kernels for 0%

profile of v1, /device:TPU:0, one launch (start us, length us, event | category | flops | bytes accessed | tf_op | source)
XLA Modules:
  0.0 82.8 jit_solution(10426935796813738792)
XLA Ops:
  0.0 0.7 convert_element_type.63
  0.7 0.7 iota_compare_fusion
  1.5 0.8 %fusion.30 = f32[8,1,8]{2,1,0:T(1,128)S(1)} fusion(bf16[8,8,128]{2,0,1:T(8,128)(2,1)} %bitcast.51, bf16[8,128,1]{1,0,2:T(8,128)(2,1)S(1)} %bitcast.48), kind=kOutput, calls=%fused_computation.34 | convolution fusion | flops 16384 | bytes 18688 | tf_op jit(solution)/shard_map/rqd,rd->rq/dot_general | solution.py:47
  2.3 4.8 %fusion.38 = (f32[8,8]{1,0:T(8,128)S(1)}, f32[8,8,3072]{2,1,0:T(8,128)S(1)}) fusion(bf16[8,1,3072,128]{3,2,1,0:T(8,128)(2,1)} %param.14, bf16[8,8,128]{2,0,1:T(8,128)(2,1)} %bitcast.52, pred[8,3072]{1,0:T(8,128)(4,1)S(1)} %iota_compare_fusion), kind=kOutput, calls=%fused_computation.46 | convolution fusion | flops 50921408 | bytes 7119104 | tf_op jit(solution)/shard_map/rqd,rtd->rqt/dot_general | solution.py:41
  7.1 0.3 fusion.19
  7.4 1.0 %fusion.16 = f32[1,8,8,128]{3,2,1,0:T(8,128)S(1)} fusion(bf16[8,1,3072,128]{3,2,1,0:T(8,128)(2,1)S(1)} %copy-done.1, f32[8,8,3072]{2,1,0:T(8,128)S(1)} %get-tuple-element.8, f32[8,8]{1,0:T(8,128)S(1)} %get-tuple-element.6, f32[8,8]{1,0:T(8,128)S(1)} %multiply_maximum_fusion, f32[8,128]{1,0:T(8,128)S(1)} %convert_element_type.63, ...), kind=kOutput, calls=%fused_computation.15 | convolution fusion | flops 50937856 | bytes 7115520 | tf_op jit(solution)/shard_map/rqt,rtd->rqd/dot_general | solution.py:55
  8.4 1.1 %broadcast_in_dim.16 = bf16[64,8,1024]{2,1,0:T(8,128)(2,1)} broadcast(bf16[8,1024]{1,0:T(8,128)(2,1)S(1)} %fusion.27), dimensions={1,2} | broadcast | bytes 1064960 | tf_op jit(solution)/shard_map/broadcast_in_dim | solution.py:64
  9.5 11.5 %all-to-all-start = ((bf16[64,8,1024]{2,1,0:T(8,128)(2,1)}), bf16[64,8,1024]{2,1,0:T(8,128)(2,1)S(1)}, u32[]{:S(2)}, u32[]{:S(2)}) async-start(bf16[64,8,1024]{2,1,0:T(8,128)(2,1)} %broadcast_in_dim.16), calls=%async_computation | async-start | bytes 2097152 | tf_op jit(solution)/shard_map/all_to_all | solution.py:65
  21.0 0.1 collective-permute-start
  21.1 0.5 collective-permute-start.1
  21.6 0.1 collective-permute-start.2
  21.7 17.9 %all-to-all-done = bf16[64,8,1024]{2,1,0:T(8,128)(2,1)S(1)} async-done(((bf16[64,8,1024]{2,1,0:T(8,128)(2,1)}), bf16[64,8,1024]{2,1,0:T(8,128)(2,1)S(1)}, u32[]{:S(2)}, u32[]{:S(2)}) %all-to-all-start) | async-done | bytes 1048608 | tf_op jit(solution)/shard_map/all_to_all | solution.py:65
  39.6 0.3 multiply_reduce_fusion
  39.9 0.1 rsqrt.12
  40.0 0.2 convert_element_type.80
  40.2 0.3 multiply_convert_fusion
  40.5 1.5 %copy-done.2 = bf16[8192,224]{0,1:T(8,128)(2,1)S(1)} copy-done((bf16[8192,224]{0,1:T(8,128)(2,1)S(1)}, bf16[8192,224]{0,1:T(8,128)(2,1)}, u32[]{:S(2)}) %copy-start.2) | copy-done | bytes 3670040
  42.0 1.3 %fusion.41 = f32[64,224]{1,0:T(8,128)S(1)} fusion(bf16[64,8192]{1,0:T(8,128)(2,1)S(1)} %multiply_convert_fusion, bf16[8192,224]{0,1:T(8,128)(2,1)S(1)} %copy-done.2), kind=kOutput, calls=%fused_computation.48 | convolution fusion | flops 234881024 | bytes 4775936 | tf_op jit(solution)/shard_map/dot_general | solution.py:78
  43.3 5.9 %fusion.12 = f32[64,8192]{1,0:T(8,128)S(1)} fusion(bf16[224,8192]{1,0:T(8,128)(2,1)} %param.21, bf16[64,8192]{1,0:T(8,128)(2,1)S(1)} %multiply_convert_fusion, bf16[8192,224]{0,1:T(8,128)(2,1)} %param.20, f32[64,224]{1,0:T(8,128)S(1)} %fusion.41), kind=kOutput, calls=%fused_computation.13 | convolution fusion | flops 469848064 | bytes 10543104 | tf_op jit(solution)/shard_map/dot_general | solution.py:81
  49.2 3.3 %fusion.42 = f32[64,224]{1,0:T(8,128)S(1)} fusion(bf16[64,8192]{1,0:T(8,128)(2,1)S(1)} %multiply_convert_fusion, bf16[8192,224]{0,1:T(8,128)(2,1)} %collective-permute-done), kind=kOutput, calls=%fused_computation.49 | convolution fusion | flops 234881024 | bytes 4775936 | tf_op jit(solution)/shard_map/dot_general | solution.py:78
  52.6 6.9 %fusion = bf16[64,8192]{1,0:T(8,128)(2,1)} fusion(f32[64,8192]{1,0:T(8,128)S(1)} %fusion.12, bf16[224,8192]{1,0:T(8,128)(2,1)} %collective-permute-done.2, f32[64,224]{1,0:T(8,128)S(1)} %fusion.42, bf16[64,8192]{1,0:T(8,128)(2,1)S(1)} %multiply_convert_fusion, bf16[8192,224]{0,1:T(8,128)(2,1)} %collective-permute-done.1), kind=kOutput, calls=%fused_computation.1 | convolution fusion | flops 470896640 | bytes 11591680 | tf_op jit(solution)/shard_map/dot_general | solution.py:81
  59.4 22.6 %all_to_all.10 = bf16[64,8,1024]{2,1,0:T(8,128)(2,1)S(1)} all-to-all(bf16[64,8,1024]{2,1,0:T(8,128)(2,1)} %bitcast.50), channel_id=1, replica_groups=mesh['role'=2,'batch'=8,'tensor'=8] {'batch','tensor'}, dimensions={0} | all-to-all | bytes 2097152 | tf_op jit(solution)/shard_map/all_to_all | solution.py:88
  82.0 0.2 convert_reduce_fusion
  82.2 0.6 add_convert_fusion
  (18 shorter events, 0.1 us)
Async XLA Ops:
  0.0 1.4 %copy-start = (bf16[8,128]{1,0:T(8,128)(2,1)S(1)}, bf16[8,128]{1,0:T(8,128)(2,1)}, u32[]{:S(2)}) copy-start(bf16[8,128]{1,0:T(8,128)(2,1)} %param.12) | copy-start | bytes 6148
  2.3 5.1 %copy-start.1 = (bf16[8,1,3072,128]{3,2,1,0:T(8,128)(2,1)S(1)}, bf16[8,1,3072,128]{3,2,1,0:T(8,128)(2,1)}, u32[]{:S(2)}) copy-start(bf16[8,1,3072,128]{3,2,1,0:T(8,128)(2,1)} %param.15) | copy-start | bytes 18874372
  7.4 1.0 %copy-start.4 = (bf16[8,1024]{1,0:T(8,128)(2,1)S(1)}, bf16[8,1024]{1,0:T(8,128)(2,1)}, u32[]{:S(2)}) copy-start(bf16[8,1024]{1,0:T(8,128)(2,1)} %param.17) | copy-start | bytes 49156
  7.4 14.3 %copy-start.3 = (bf16[8192]{0:T(1024)(128)(2,1)S(1)}, bf16[8192]{0:T(1024)(128)(2,1)}, u32[]{:S(2)}) copy-start(bf16[8192]{0:T(1024)(128)(2,1)} %param.18) | copy-start | bytes 49156
  9.5 30.1 %all-to-all-start = ((bf16[64,8,1024]{2,1,0:T(8,128)(2,1)}), bf16[64,8,1024]{2,1,0:T(8,128)(2,1)S(1)}, u32[]{:S(2)}, u32[]{:S(2)}) async-start(bf16[64,8,1024]{2,1,0:T(8,128)(2,1)} %broadcast_in_dim.16), calls=%async_computation | async-start | bytes 2097152 | tf_op jit(solution)/shard_map/all_to_all | solution.py:65
  21.0 28.2 %collective-permute-start = (bf16[8192,224]{0,1:T(8,128)(2,1)}, bf16[8192,224]{0,1:T(8,128)(2,1)}, u32[]{:S(2)}, u32[]{:S(2)}) collective-permute-start(bf16[8192,224]{0,1:T(8,128)(2,1)} %param.19), channel_id=1, source_target_pairs={{0,64},{64,0},{1,65},{65,1},{2,66},{66,2},{3,67},{67,3},{4,68},{68... | collective-permute-start | bytes 11010056 | tf_op jit(solution)/shard_map/ppermute | solution.py:32
  21.1 31.4 %collective-permute-start.1 = (bf16[8192,224]{0,1:T(8,128)(2,1)}, bf16[8192,224]{0,1:T(8,128)(2,1)}, u32[]{:S(2)}, u32[]{:S(2)}) collective-permute-start(bf16[8192,224]{0,1:T(8,128)(2,1)} %param.20), channel_id=1, source_target_pairs={{0,64},{64,0},{1,65},{65,1},{2,66},{66,2},{3,67},{67,3},{4,68},{68... | collective-permute-start | bytes 11010056 | tf_op jit(solution)/shard_map/ppermute | solution.py:33
  21.6 31.0 %collective-permute-start.2 = (bf16[224,8192]{1,0:T(8,128)(2,1)}, bf16[224,8192]{1,0:T(8,128)(2,1)}, u32[]{:S(2)}, u32[]{:S(2)}) collective-permute-start(bf16[224,8192]{1,0:T(8,128)(2,1)} %param.21), channel_id=1, source_target_pairs={{0,64},{64,0},{1,65},{65,1},{2,66},{66,2},{3,67},{67,3},{4,68},{68... | collective-permute-start | bytes 11010056 | tf_op jit(solution)/shard_map/ppermute | solution.py:34
  40.0 2.0 %copy-start.2 = (bf16[8192,224]{0,1:T(8,128)(2,1)S(1)}, bf16[8192,224]{0,1:T(8,128)(2,1)}, u32[]{:S(2)}) copy-start(bf16[8192,224]{0,1:T(8,128)(2,1)} %param.19) | copy-start | bytes 11010052

commit v2 on v1

v2 whole, which is shorter than its diff:
```python
import functools

import jax
import jax.numpy as jnp
from jax import lax
from jax.experimental import pallas as pl
from jax.experimental.pallas import tpu as pltpu
from jax.sharding import PartitionSpec as P

AXES = ("role", "batch", "tensor")
CHIPS = ("batch", "tensor")
CHUNK = 1024
TOGETHER = 4
STEP = 2048
CONTRACT_LAST = (((1,), (1,)), ((), ()))
F32 = jnp.float32
BF16 = jnp.bfloat16
HBM = pl.BlockSpec(memory_space=pltpu.HBM)
VMEM = pl.BlockSpec(memory_space=pltpu.VMEM)


def in_hbm(array):
    return pltpu.with_memory_space_constraint(array, pltpu.HBM)


def attention_kernel(
    lengths_hbm,
    queries_hbm,
    new_keys_hbm,
    new_values_hbm,
    residual_hbm,
    keys_hbm,
    values_hbm,
    hidden_out,
    copies_out,
    lengths,
    queries,
    new_keys,
    new_values,
    residual,
    keys,
    values,
    heads,
    probs,
    mixed,
    small_sems,
    sems,
):
    rows, group, head = heads.shape
    cache_len = keys.shape[1]
    chunks = cache_len // CHUNK
    copies = copies_out.shape[0]

    def copy(which, row, chunk):
        source, target = ((keys_hbm, keys), (values_hbm, values))[which]
        span = pl.ds(chunk * CHUNK, CHUNK)
        return pltpu.make_async_copy(
            source.at[row, 0, span], target.at[row, span], sems.at[which, row, chunk]
        )

    def used(row, chunk):
        return chunk * CHUNK < lengths[row]

    small = [
        pltpu.make_async_copy(source, target, small_sems.at[i])
        for i, (source, target) in enumerate(
            (
                (lengths_hbm, lengths),
                (queries_hbm, queries),
                (new_keys_hbm, new_keys),
                (new_values_hbm, new_values),
                (residual_hbm, residual),
            )
        )
    ]
    for one in small:
        one.start()
    for which in range(2):
        for row in range(rows):
            copy(which, row, 0).start()
    small[0].wait()
    for which in range(2):
        for row in range(rows):
            for chunk in range(1, chunks):

                @pl.when(used(row, chunk))
                def _():
                    copy(which, row, chunk).start()

    for one in small[1:]:
        one.wait()

    def arrive(which, first):
        for row in range(first, first + TOGETHER):
            copy(which, row, 0).wait()
            for chunk in range(1, chunks):

                @pl.when(used(row, chunk))
                def _():
                    copy(which, row, chunk).wait()

    factor = head ** (-0.5)
    for j in range(group):
        heads[:, j, :] = queries[:, j * head : (j + 1) * head].astype(F32)
    own_scores = (
        jnp.sum(heads[...] * new_keys[...].astype(F32)[:, None, :], axis=-1, keepdims=True)
        * factor
    )
    place = lax.broadcasted_iota(jnp.int32, (group, cache_len), 1)
    own_probs = []
    for first in range(0, rows, TOGETHER):
        arrive(0, first)
        for row in range(first, first + TOGETHER):
            products = lax.dot_general(
                heads[row].astype(BF16), keys[row], CONTRACT_LAST, preferred_element_type=F32
            )
            scores = jnp.where(place < lengths[row], products * factor, -jnp.inf)
            own = own_scores[row]
            top = jnp.maximum(jnp.max(scores, axis=-1, keepdims=True), own)
            weights = jnp.exp(scores - top)
            own_weight = jnp.exp(own - top)
            denominator = jnp.sum(weights, axis=-1, keepdims=True) + own_weight
            probs[row] = (weights / denominator).astype(BF16)
            own_probs.append((own_weight / denominator).astype(BF16).astype(F32))

    for first in range(0, rows, TOGETHER):
        arrive(1, first)
        for row in range(first, first + TOGETHER):
            total = own_probs[row] * new_values[row : row + 1, :].astype(F32)
            for chunk in range(chunks):
                span = slice(chunk * CHUNK, (chunk + 1) * CHUNK)
                part = values[row, span, :]
                if chunk:
                    part = jnp.where(used(row, chunk), part, jnp.zeros_like(part))
                total += jnp.dot(probs[row, :, span], part, preferred_element_type=F32)
            mixed[row] = total

    for j in range(group):
        span = slice(j * head, (j + 1) * head)
        hidden = (residual[:, span].astype(F32) + mixed[:, j, :]).astype(BF16)
        hidden_out[:, span] = hidden
        for k in range(copies):
            copies_out[k, :, span] = hidden


def attention(queries, new_keys, new_values, key_cache, value_cache, lengths, residual, copies):
    rows, width = queries.shape
    head = new_keys.shape[1]
    group = width // head
    cache_len = key_cache.shape[2]
    operands = (lengths, queries, new_keys, new_values, residual, key_cache, value_cache)
    return pl.pallas_call(
        attention_kernel,
        out_shape=(
            jax.ShapeDtypeStruct((rows, width), BF16),
            jax.ShapeDtypeStruct((copies, rows, width), BF16),
        ),
        in_specs=[HBM] * len(operands),
        out_specs=(VMEM, VMEM),
        scratch_shapes=[
            pltpu.SMEM((rows,), jnp.int32),
            pltpu.VMEM((rows, width), BF16),
            pltpu.VMEM((rows, head), BF16),
            pltpu.VMEM((rows, head), BF16),
            pltpu.VMEM((rows, width), BF16),
            pltpu.VMEM((rows, cache_len, head), BF16),
            pltpu.VMEM((rows, cache_len, head), BF16),
            pltpu.VMEM((rows, group, head), F32),
            pltpu.VMEM((rows, group, cache_len), BF16),
            pltpu.VMEM((rows, group, head), F32),
            pltpu.SemaphoreType.DMA((5,)),
            pltpu.SemaphoreType.DMA((2, rows, cache_len // CHUNK)),
        ],
        compiler_params=pltpu.CompilerParams(vmem_limit_bytes=24 << 20),
        cost_estimate=pl.CostEstimate(
            flops=4 * rows * group * cache_len * head,
            bytes_accessed=4 * rows * cache_len * head,
            transcendentals=rows * group * cache_len,
        ),
        name="attention",
    )(*(in_hbm(x) for x in operands))


def feed_forward_kernel(batch, tensor, pieces, gain, *refs):
    mate = refs[:3]
    own_hbm = refs[3:6]
    out, normed = refs[6:8]
    own = refs[8:11]
    sems = refs[11]
    rows, width = pieces.shape[1:]
    units, features = own[0].shape
    steps = features // STEP

    def span_of(step):
        return slice(step * STEP, (step + 1) * STEP)

    arrivals = []
    for which in ((0, 1), (2,)):
        for step in range(steps):
            arrivals.append(
                [
                    pltpu.make_async_copy(
                        own_hbm[w].at[:, span_of(step)],
                        own[w].at[:, span_of(step)],
                        sems.at[w, step],
                    )
                    for w in which
                ]
            )
    for group in arrivals:
        for one in group:
            one.start()

    for pair in range(batch // 2):
        inverse = []
        for half in range(2):
            start = (pair * 2 + half) * tensor
            total = jnp.zeros((rows, width), F32)
            for t in range(tensor):
                part = pieces[start + t].astype(F32)
                total = total + part * part
            mean_square = jnp.sum(total, axis=-1, keepdims=True) * (1.0 / features)
            inverse.append(lax.rsqrt(mean_square + 1e-05))
        for t in range(tensor):
            lanes = gain.shape[1]
            tiles = width // lanes
            scale = jnp.concatenate(
                [gain[t * tiles + i : t * tiles + i + 1, :].astype(F32) for i in range(tiles)],
                axis=1,
            )
            parts = [
                pieces[(pair * 2 + half) * tensor + t].astype(F32) * inverse[half] * scale
                for half in range(2)
            ]
            normed[pair * 2 * rows : (pair + 1) * 2 * rows, t * width : (t + 1) * width] = (
                jnp.concatenate(parts, axis=0).astype(BF16)
            )

    def project(weights, arrived):
        sums = [jnp.zeros((units, batch * rows), F32) for _ in range(2)]
        for step in range(steps):
            for one in arrived[step]:
                one.wait()
            block = normed[:, span_of(step)]
            for i in range(2):
                sums[i] += lax.dot_general(
                    weights[i][:, span_of(step)],
                    block,
                    CONTRACT_LAST,
                    preferred_element_type=F32,
                )
        gate, up = sums
        return (gate / (1.0 + jnp.exp(-gate)) * up).astype(BF16).T

    active_mate = project(mate, [()] * steps)
    active_own = project(own, arrivals[:steps])
    for step in range(steps):
        span = span_of(step)
        partial = jnp.dot(active_mate, mate[2][:, span], preferred_element_type=F32)
        for one in arrivals[steps + step]:
            one.wait()
        partial += jnp.dot(active_own, own[2][:, span], preferred_element_type=F32)
        for i in range(STEP // width):
            t = step * (STEP // width) + i
            for b in range(batch):
                out[b * tensor + t] = partial[
                    b * rows : (b + 1) * rows, i * width : (i + 1) * width
                ].astype(BF16)


def feed_forward(pieces, gain, own, mate, batch, tensor):
    rows, width = pieces.shape[1:]
    features = tensor * width
    units = own[2].shape[0]
    own = [in_hbm(w) for w in (own[0].T, own[1].T, own[2])]
    mate = [mate[0].T, mate[1].T, mate[2]]
    return pl.pallas_call(
        functools.partial(feed_forward_kernel, batch, tensor),
        out_shape=jax.ShapeDtypeStruct(pieces.shape, BF16),
        in_specs=[VMEM] * 5 + [HBM] * 3,
        out_specs=VMEM,
        scratch_shapes=[pltpu.VMEM((batch * rows, features), BF16)]
        + [pltpu.VMEM((units, features), BF16)] * 3
        + [pltpu.SemaphoreType.DMA((3, features // STEP))],
        compiler_params=pltpu.CompilerParams(vmem_limit_bytes=24 << 20),
        cost_estimate=pl.CostEstimate(
            flops=12 * batch * rows * units * features,
            bytes_accessed=12 * units * features,
            transcendentals=2 * batch * rows * units,
        ),
        name="feed_forward",
    )(pieces, gain.reshape(features // 128, 128), *mate, *own)


def local(
    queries,
    new_keys,
    new_values,
    key_cache,
    value_cache,
    lengths,
    residual,
    norm_gain,
    gate_weight,
    up_weight,
    down_weight,
):
    batch = lax.axis_size("batch")
    tensor = lax.axis_size("tensor")
    own = (gate_weight, up_weight, down_weight)
    mate = tuple(lax.ppermute(w, "role", [(0, 1), (1, 0)]) for w in own)
    hidden_state, copies = attention(
        queries, new_keys, new_values, key_cache, value_cache, lengths, residual, batch * tensor
    )
    pieces = lax.all_to_all(copies, CHIPS, 0, 0, tiled=True)
    partial_out = feed_forward(pieces, norm_gain, own, mate, batch, tensor)
    received = lax.all_to_all(partial_out, CHIPS, 0, 0, tiled=True)
    summed = jnp.sum(received.astype(F32), axis=0)
    return (hidden_state.astype(F32) + summed).astype(BF16)


def solution(mesh):
    rows = ("role", "batch")
    in_specs = (
        P(rows, "tensor"),
        P(rows, "tensor"),
        P(rows, "tensor"),
        P(rows, "tensor", None, None),
        P(rows, "tensor", None, None),
        P(rows),
        P(rows, "tensor"),
        P(),
        P(None, AXES),
        P(None, AXES),
        P(AXES, None),
    )
    return jax.shard_map(
        local, mesh=mesh, in_specs=in_specs, out_specs=P(rows, "tensor"), check_vma=False
    )
```

time: 83.2 us -> 69.4 us (0.83)
  blocking collectives: 22.6 us -> 52.7 us
  matrix products: 24 us -> 0 us
  waiting for transfers between devices: 17.9 us -> 0.01 us
  Pallas kernels: 0 us -> 15.2 us
  starting transfers between devices: 12.2 us -> 0.51 us
  local copies, waits for them, and re-layouts: 2.7 us -> 0.01 us
  other arithmetic: 3.37 us -> 0.79 us
    all_to_all x1 -> x2, blocking collectives: 22.6 us -> 52.7 us  [the longest x1 29.9 us: local(): pieces = lax.all_to_all(copies, CHIPS, 0, 0, tiled=True)]
    dot_general x7 -> x0, matrix products: 24 us -> none  [the longest x2 12.8 us: local(): jnp.dot(activation, down_part, preferred_element_type=jnp.float32)]
    all_to_all x1 -> x0, waiting for transfers between devices: 17.9 us -> none  [local(): pieces = lax.all_to_all(copies, CHIPS, 0, 0, tiled=True)]
    pallas_call x0 -> x2, Pallas kernels: none -> 15.2 us  [the longest x1 8.39 us: feed_forward(): pl.pallas_call(functools.partial(feed_forward_kernel, batch, tensor), out...]
    all_to_all x1 -> x0, starting transfers between devices: 11.5 us -> none  [local(): pieces = lax.all_to_all(copies, CHIPS, 0, 0, tiled=True)]
    unnamed x10 -> x2, local copies, waits for them, and re-layouts: 1.52 us -> 0.01 us
    convert_element_type x7 -> x1, other arithmetic: 1.88 us -> 0.61 us  [local(): return (hidden_state.astype(F32) + summed).astype(BF16)]
    broadcast_in_dim x1 -> x0, local copies, waits for them, and re-layouts: 1.1 us -> none  [local(): copies = jnp.broadcast_to(hidden_state[None], (chips, local_rows, width))]
  transfers between devices with their start and end apart: 4 -> 3, of which waited for: 1 -> 0; matrix products, arithmetic and copies ran while one was open for 14% -> 0% of each run, Pallas kernels for 0% -> 10%
where the time goes in v2:
time: 69.4 us; the launch traced here: 69.2 us
  blocking collectives  52.7 us (76%)
  Pallas kernels  15.2 us (22%)
  other arithmetic  0.79 us (1%)
    all_to_all x1, blocking collectives, local(): pieces = lax.all_to_all(copies, CHIPS, 0, 0, tiled=True)  29.9 us
    all_to_all x1, blocking collectives, local(): received = lax.all_to_all(partial_out, CHIPS, 0, 0, tiled=True)  22.7 us
    pallas_call x1, Pallas kernels, feed_forward(): pl.pallas_call(functools.partial(feed_forward_kernel, batch, tensor), out...  8.39 us
    pallas_call x1, Pallas kernels, attention(): pl.pallas_call(attention_kernel, out_shape=(jax.ShapeDtypeStruct((rows, w...  6.82 us
  transfers between devices with their start and end apart: 3, of which 0 were waited for; matrix products, arithmetic and copies ran while one was open for 0% of the time, Pallas kernels for 10%

profile of v2, /device:TPU:0, one launch (start us, length us, event | category | flops | bytes accessed | tf_op | source)
XLA Modules:
  0.0 69.2 jit_solution(12998741461808750607)
XLA Ops:
  0.0 0.0 copy-start
  0.0 0.0 collective-permute-start
  0.0 0.5 collective-permute-start.1
  0.5 0.0 collective-permute-start.2
  0.5 6.8 %attention.1 = (bf16[8,1024]{1,0:T(8,128)(2,1)S(1)}, bf16[64,8,1024]{2,1,0:T(8,128)(2,1)S(1)}) custom-call(s32[8]{0:T(128)} %lengths_hbm.1, bf16[8,1024]{1,0:T(8,128)(2,1)} %queries_hbm.1, bf16[8,128]{1,0:T(8,128)(2,1)} %new_keys_hbm.1, bf16[8,128]{1,0:T(8,128)(2,1)} %new_values_hbm.1, bf16[8,1024]{1,0:T(8,128)(2,1)} %residual_hbm.1, ...), custom_call_target="tpu_custom_call" | custom-call | flops 100663296 | bytes 12582912 | tf_op jit(solution)/shard_map/attention/pallas_call | solution.py:152
  7.3 29.9 %all_to_all.10.pieces = bf16[64,8,1024]{2,1,0:T(8,128)(2,1)S(1)} all-to-all(bf16[64,8,1024]{2,1,0:T(8,128)(2,1)S(1)} %get-tuple-element.8), channel_id=1, replica_groups=mesh['role'=2,'batch'=8,'tensor'=8] {'batch','tensor'}, dimensions={0} | all-to-all | bytes 2097152 | tf_op jit(solution)/shard_map/all_to_all | solution.py:315
  37.3 0.0 collective-permute-done
  37.3 0.0 collective-permute-done.1
  37.3 0.0 collective-permute-done.2.refs_2_
  37.3 0.0 copy-done
  37.3 8.4 %feed_forward.1 = bf16[64,8,1024]{2,1,0:T(8,128)(2,1)S(1)} custom-call(bf16[64,8,1024]{2,1,0:T(8,128)(2,1)S(1)} %all_to_all.10.pieces, bf16[64,128]{1,0:T(8,128)(2,1)S(1)} %bitcast.7, bf16[224,8192]{1,0:T(8,128)(2,1)S(1)} %bitcast.5, bf16[224,8192]{1,0:T(8,128)(2,1)S(1)} %bitcast.6, bf16[224,8192]{1,0:T(8,128)(2,1)S(1)} %collective-permute-done.2.refs_2_, ...), custom_call_target="tpu_custom_call" | custom-call | flops 1409286144 | bytes 22020096 | tf_op jit(solution)/shard_map/feed_forward/pallas_call | solution.py:277
  45.7 22.7 %all_to_all.11 = bf16[64,8,1024]{2,1,0:T(8,128)(2,1)S(1)} all-to-all(bf16[64,8,1024]{2,1,0:T(8,128)(2,1)S(1)} %feed_forward.1), channel_id=1, replica_groups=mesh['role'=2,'batch'=8,'tensor'=8] {'batch','tensor'}, dimensions={0} | all-to-all | bytes 2097152 | tf_op jit(solution)/shard_map/all_to_all | solution.py:317
  68.4 0.2 convert_reduce_fusion
  68.6 0.6 add_convert_fusion
Async XLA Ops:
  0.0 37.3 %copy-start = (bf16[8192]{0:T(1024)(128)(2,1)S(1)}, bf16[8192]{0:T(1024)(128)(2,1)}, u32[]{:S(2)}) copy-start(bf16[8192]{0:T(1024)(128)(2,1)} %param.18) | copy-start | bytes 49156
  0.0 37.3 %collective-permute-start = (bf16[8192,224]{0,1:T(8,128)(2,1)}, bf16[8192,224]{0,1:T(8,128)(2,1)S(1)}, u32[]{:S(2)}, u32[]{:S(2)}) collective-permute-start(bf16[8192,224]{0,1:T(8,128)(2,1)} %param.19), channel_id=1, source_target_pairs={{0,64},{64,0},{1,65},{65,1},{2,66},{66,2},{3,67},{67,3},{4,68},{68... | collective-permute-start | bytes 11010056 | tf_op jit(solution)/shard_map/ppermute | solution.py:311
  0.0 37.3 %collective-permute-start.1 = (bf16[8192,224]{0,1:T(8,128)(2,1)}, bf16[8192,224]{0,1:T(8,128)(2,1)S(1)}, u32[]{:S(2)}, u32[]{:S(2)}) collective-permute-start(bf16[8192,224]{0,1:T(8,128)(2,1)} %param.20), channel_id=1, source_target_pairs={{0,64},{64,0},{1,65},{65,1},{2,66},{66,2},{3,67},{67,3},{4,68},{68... | collective-permute-start | bytes 11010056 | tf_op jit(solution)/shard_map/ppermute | solution.py:311
  0.5 36.8 %collective-permute-start.2 = (bf16[224,8192]{1,0:T(8,128)(2,1)}, bf16[224,8192]{1,0:T(8,128)(2,1)S(1)}, u32[]{:S(2)}, u32[]{:S(2)}) collective-permute-start(bf16[224,8192]{1,0:T(8,128)(2,1)} %refs_5_.1), channel_id=1, source_target_pairs={{0,64},{64,0},{1,65},{65,1},{2,66},{66,2},{3,67},{67,3},{4,68},{68... | collective-permute-start | bytes 11010056 | tf_op jit(solution)/shard_map/ppermute | solution.py:311

commit v3 on v2

v3 whole, which is shorter than its diff:
```python
import functools

import jax
import jax.numpy as jnp
from jax import lax
from jax.experimental import pallas as pl
from jax.experimental.pallas import tpu as pltpu
from jax.sharding import PartitionSpec as P

AXES = ("role", "batch", "tensor")
CHIPS = ("batch", "tensor")
PACK = 16
TOGETHER = 4
STAGE_AFTER = 0
STEP = 4096
CONTRACT_LAST = (((1,), (1,)), ((), ()))
F32 = jnp.float32
BF16 = jnp.bfloat16
HBM = pl.BlockSpec(memory_space=pltpu.HBM)
VMEM = pl.BlockSpec(memory_space=pltpu.VMEM)


def in_hbm(array):
    return pltpu.with_memory_space_constraint(array, pltpu.HBM)


def attention_kernel(
    lengths_hbm,
    queries_hbm,
    new_keys_hbm,
    new_values_hbm,
    residual_hbm,
    keys_hbm,
    values_hbm,
    gate_hbm,
    up_hbm,
    hidden_out,
    copies_out,
    gate_out,
    up_out,
    lengths,
    queries,
    new_keys,
    new_values,
    residual,
    keys,
    values,
    heads,
    probs,
    mixed,
    small_sems,
    sems,
    stage_sems,
):
    rows, group, head = heads.shape
    cache_len = keys.shape[1]
    copies = copies_out.shape[0]

    def copy(which, row):
        source, target = ((keys_hbm, keys), (values_hbm, values))[which]
        length = (lengths[row] + PACK - 1) // PACK * PACK
        span = pl.ds(0, pl.multiple_of(length, PACK))
        return pltpu.make_async_copy(
            source.at[row, 0, span], target.at[row, span], sems.at[which, row]
        )

    small = [
        pltpu.make_async_copy(source, target, small_sems.at[i])
        for i, (source, target) in enumerate(
            (
                (lengths_hbm, lengths),
                (queries_hbm, queries),
                (new_keys_hbm, new_keys),
                (new_values_hbm, new_values),
                (residual_hbm, residual),
            )
        )
    ]
    for one in small:
        one.start()
    for row in range(rows):
        values[row] = jnp.zeros((cache_len, head), BF16)
    small[0].wait()
    for which in range(2):
        for row in range(rows):
            copy(which, row).start()
    for one in small[1:]:
        one.wait()

    staged = [
        pltpu.make_async_copy(gate_hbm, gate_out, stage_sems.at[0]),
        pltpu.make_async_copy(up_hbm, up_out, stage_sems.at[1]),
    ]
    factor = head ** (-0.5)
    for j in range(group):
        heads[:, j, :] = queries[:, j * head : (j + 1) * head].astype(F32)
    own_scores = (
        jnp.sum(heads[...] * new_keys[...].astype(F32)[:, None, :], axis=-1, keepdims=True)
        * factor
    )
    place = lax.broadcasted_iota(jnp.int32, (group, cache_len), 1)
    own_probs = []
    for first in range(0, rows, TOGETHER):
        for row in range(first, first + TOGETHER):
            copy(0, row).wait()
        if first == STAGE_AFTER:
            for one in staged:
                one.start()
        for row in range(first, first + TOGETHER):
            products = lax.dot_general(
                heads[row].astype(BF16), keys[row], CONTRACT_LAST, preferred_element_type=F32
            )
            scores = jnp.where(place < lengths[row], products * factor, -jnp.inf)
            own = own_scores[row]
            top = jnp.maximum(jnp.max(scores, axis=-1, keepdims=True), own)
            weights = jnp.exp(scores - top)
            own_weight = jnp.exp(own - top)
            denominator = jnp.sum(weights, axis=-1, keepdims=True) + own_weight
            probs[row] = (weights / denominator).astype(BF16)
            own_probs.append((own_weight / denominator).astype(BF16).astype(F32))

    for first in range(0, rows, TOGETHER):
        for row in range(first, first + TOGETHER):
            copy(1, row).wait()
        for row in range(first, first + TOGETHER):
            total = own_probs[row] * new_values[row : row + 1, :].astype(F32)
            total += jnp.dot(probs[row], values[row], preferred_element_type=F32)
            mixed[row] = total

    for j in range(group):
        span = slice(j * head, (j + 1) * head)
        hidden = (residual[:, span].astype(F32) + mixed[:, j, :]).astype(BF16)
        hidden_out[:, span] = hidden
        for k in range(copies):
            copies_out[k, :, span] = hidden
    for one in staged:
        one.wait()


def attention(
    queries,
    new_keys,
    new_values,
    key_cache,
    value_cache,
    lengths,
    residual,
    copies,
    gate,
    up,
):
    rows, width = queries.shape
    head = new_keys.shape[1]
    group = width // head
    cache_len = key_cache.shape[2]
    operands = (
        lengths,
        queries,
        new_keys,
        new_values,
        residual,
        key_cache,
        value_cache,
        gate,
        up,
    )
    return pl.pallas_call(
        attention_kernel,
        out_shape=(
            jax.ShapeDtypeStruct((rows, width), BF16),
            jax.ShapeDtypeStruct((copies, rows, width), BF16),
            jax.ShapeDtypeStruct(gate.shape, BF16),
            jax.ShapeDtypeStruct(up.shape, BF16),
        ),
        in_specs=[HBM] * len(operands),
        out_specs=(VMEM,) * 4,
        scratch_shapes=[
            pltpu.SMEM((rows,), jnp.int32),
            pltpu.VMEM((rows, width), BF16),
            pltpu.VMEM((rows, head), BF16),
            pltpu.VMEM((rows, head), BF16),
            pltpu.VMEM((rows, width), BF16),
            pltpu.VMEM((rows, cache_len, head), BF16),
            pltpu.VMEM((rows, cache_len, head), BF16),
            pltpu.VMEM((rows, group, head), F32),
            pltpu.VMEM((rows, group, cache_len), BF16),
            pltpu.VMEM((rows, group, head), F32),
            pltpu.SemaphoreType.DMA((5,)),
            pltpu.SemaphoreType.DMA((2, rows)),
            pltpu.SemaphoreType.DMA((2,)),
        ],
        compiler_params=pltpu.CompilerParams(vmem_limit_bytes=24 << 20),
        cost_estimate=pl.CostEstimate(
            flops=4 * rows * group * cache_len * head,
            bytes_accessed=4 * rows * cache_len * head,
            transcendentals=rows * group * cache_len,
        ),
        name="attention",
    )(*(in_hbm(x) for x in operands))


def feed_forward_kernel(batch, tensor, place, pieces, gain, *refs):
    mate, (own_gate, own_up, down_hbm) = refs[:3], refs[3:6]
    out, normed, own_down, sems = refs[6:]
    rows, width = pieces.shape[1:]
    units, features = own_gate.shape
    arrivals = []
    for i, start in enumerate(range(0, features, STEP)):
        span = pl.ds(start, STEP)
        arrivals.append(
            pltpu.make_async_copy(down_hbm.at[:, span], own_down.at[:, span], sems.at[i])
        )
        arrivals[-1].start()
    lanes = gain.shape[1]
    tiles = width // lanes

    for pair in range(batch // 2):
        inverse = []
        for half in range(2):
            total = jnp.zeros((rows, width), F32)
            for t in range(tensor):
                part = pieces[place[(pair * 2 + half) * tensor + t]].astype(F32)
                total = total + part * part
            mean_square = jnp.sum(total, axis=-1, keepdims=True) * (1.0 / features)
            inverse.append(lax.rsqrt(mean_square + 1e-05))
        for t in range(tensor):
            scale = jnp.concatenate(
                [gain[t * tiles + i : t * tiles + i + 1, :].astype(F32) for i in range(tiles)],
                axis=1,
            )
            parts = [
                pieces[place[(pair * 2 + half) * tensor + t]].astype(F32) * inverse[half] * scale
                for half in range(2)
            ]
            normed[pair * 2 * rows : (pair + 1) * 2 * rows, t * width : (t + 1) * width] = (
                jnp.concatenate(parts, axis=0).astype(BF16)
            )

    def project(weights):
        sums = [jnp.zeros((units, batch * rows), F32) for _ in range(2)]
        for start in range(0, features, STEP):
            span = slice(start, start + STEP)
            block = normed[:, span]
            for i in range(2):
                sums[i] += lax.dot_general(
                    weights[i][:, span], block, CONTRACT_LAST, preferred_element_type=F32
                )
        gate, up = sums
        return (gate / (1.0 + jnp.exp(-gate)) * up).astype(BF16).T

    active_own = project((own_gate, own_up))
    active_mate = project(mate[:2])
    for one, start in zip(arrivals, range(0, features, STEP)):
        span = slice(start, start + STEP)
        partial = jnp.dot(active_mate, mate[2][:, span], preferred_element_type=F32)
        one.wait()
        partial += jnp.dot(active_own, own_down[:, span], preferred_element_type=F32)
        for i in range(STEP // width):
            t = start // width + i
            for b in range(batch):
                out[place[b * tensor + t]] = partial[
                    b * rows : (b + 1) * rows, i * width : (i + 1) * width
                ].astype(BF16)


def feed_forward(pieces, gain, own, mate, batch, tensor, place):
    rows, width = pieces.shape[1:]
    features = tensor * width
    units = own[2].shape[0]
    return pl.pallas_call(
        functools.partial(feed_forward_kernel, batch, tensor, place),
        out_shape=jax.ShapeDtypeStruct(pieces.shape, BF16),
        in_specs=[VMEM] * 7 + [HBM],
        out_specs=VMEM,
        scratch_shapes=[
            pltpu.VMEM((batch * rows, features), BF16),
            pltpu.VMEM((units, features), BF16),
            pltpu.SemaphoreType.DMA((features // STEP,)),
        ],
        compiler_params=pltpu.CompilerParams(vmem_limit_bytes=16 << 20),
        cost_estimate=pl.CostEstimate(
            flops=12 * batch * rows * units * features,
            bytes_accessed=12 * units * features,
            transcendentals=2 * batch * rows * units,
        ),
        name="feed_forward",
    )(pieces, gain.reshape(features // 128, 128), *mate, own[0], own[1], in_hbm(own[2]))


def chip_order(batch, tensor):
    side = round((batch * tensor) ** (1 / 3))
    order = []
    for step in range(batch * tensor):
        at = 21 * step % (batch * tensor)
        x, y, z = at % side, at // side % side, at // (side * side)
        half = side // 2
        order.append((y % half * side + x) * tensor + z * half + y // half)
    return order


def local(
    queries,
    new_keys,
    new_values,
    key_cache,
    value_cache,
    lengths,
    residual,
    norm_gain,
    gate_weight,
    up_weight,
    down_weight,
):
    batch = lax.axis_size("batch")
    tensor = lax.axis_size("tensor")
    chips = batch * tensor
    order = chip_order(batch, tensor)
    place = [order.index(chip) for chip in range(chips)]
    groups = [[role * chips + chip for chip in order] for role in range(2)]
    exchange = functools.partial(
        lax.all_to_all,
        axis_name=AXES,
        split_axis=0,
        concat_axis=0,
        tiled=True,
        axis_index_groups=groups,
    )
    own = (gate_weight.T, up_weight.T, down_weight)
    mate = tuple(lax.ppermute(w, "role", [(0, 1), (1, 0)]) for w in own)
    hidden_state, copies, *near = attention(
        queries,
        new_keys,
        new_values,
        key_cache,
        value_cache,
        lengths,
        residual,
        chips,
        own[0],
        own[1],
    )
    pieces = exchange(copies)
    own = (*near, own[2])
    partial_out = feed_forward(pieces, norm_gain, own, mate, batch, tensor, place)
    received = exchange(partial_out)
    summed = jnp.sum(received.astype(F32), axis=0)
    return (hidden_state.astype(F32) + summed).astype(BF16)


def solution(mesh):
    rows = ("role", "batch")
    in_specs = (
        P(rows, "tensor"),
        P(rows, "tensor"),
        P(rows, "tensor"),
        P(rows, "tensor", None, None),
        P(rows, "tensor", None, None),
        P(rows),
        P(rows, "tensor"),
        P(),
        P(None, AXES),
        P(None, AXES),
        P(AXES, None),
    )
    return jax.shard_map(
        local, mesh=mesh, in_specs=in_specs, out_specs=P(rows, "tensor"), check_vma=False
    )
```

time: 69.4 us -> 66.3 us (0.955)
  blocking collectives: 52.7 us -> 51 us
  Pallas kernels: 15.2 us -> 13.8 us
    all_to_all x2, blocking collectives: 52.7 us -> 51 us  [the longest x1 27.9 us: local(): pieces = exchange(copies)]
    pallas_call x1, Pallas kernels: 8.39 us -> 7.12 us  [feed_forward(): pl.pallas_call(functools.partial(feed_forward_kernel, batch, tensor, plac...]
where the time goes in v3:
time: 66.3 us; the launch traced here: 66.1 us
  blocking collectives  51 us (77%)
  Pallas kernels  13.8 us (21%)
  other arithmetic  0.78 us (1%)
    all_to_all x1, blocking collectives, local(): pieces = exchange(copies)  27.9 us
    all_to_all x1, blocking collectives, local(): received = exchange(partial_out)  23 us
    pallas_call x1, Pallas kernels, feed_forward(): pl.pallas_call(functools.partial(feed_forward_kernel, batch, tensor, plac...  7.12 us
    pallas_call x1, Pallas kernels, attention(): pl.pallas_call(attention_kernel, out_shape=(jax.ShapeDtypeStruct((rows, w...  6.7 us
  transfers between devices with their start and end apart: 3, of which 0 were waited for; matrix products, arithmetic and copies ran while one was open for 0% of the time, Pallas kernels for 10%

profile of v3, /device:TPU:0, one launch (start us, length us, event | category | flops | bytes accessed | tf_op | source)
XLA Modules:
  0.0 66.1 jit_solution(1706275925620002004)
XLA Ops:
  0.0 0.0 collective-permute-start
  0.0 0.0 copy-start
  0.0 0.5 collective-permute-start.1
  0.5 0.0 collective-permute-start.2
  0.5 6.7 %attention.1 = (bf16[8,1024]{1,0:T(8,128)(2,1)S(1)}, bf16[64,8,1024]{2,1,0:T(8,128)(2,1)S(1)}, bf16[224,8192]{1,0:T(8,128)(2,1)S(1)}, bf16[224,8192]{1,0:T(8,128)(2,1)S(1)}) custom-call(s32[8]{0:T(128)} %lengths_hbm.1, bf16[8,1024]{1,0:T(8,128)(2,1)} %queries_hbm.1, bf16[8,128]{1,0:T(8,128)(2,1)} %new_keys_hbm.1, bf16[8,128]{1,0:T(8,128)(2,1)} %new_values_hbm.1, ...), custom_call_target="tpu_custom_call" | custom-call | flops 100663296 | bytes 12582912 | tf_op jit(solution)/shard_map/attention/pallas_call | solution.py:167
  7.2 27.9 %all_to_all.10.pieces = bf16[64,8,1024]{2,1,0:T(8,128)(2,1)S(1)} all-to-all(bf16[64,8,1024]{2,1,0:T(8,128)(2,1)S(1)} %get-tuple-element.10), channel_id=1, replica_groups={{0,42,21,63,34,13,55,26,5,47,18,60,39,10,52,31,2,44,23,57,36,15,49,28,7..., dimensions={0} | all-to-all | bytes 2097152 | tf_op jit(solution)/shard_map/all_to_all | solution.py:342
  35.2 0.0 collective-permute-done.refs_0_
  35.2 0.0 collective-permute-done.1.refs_1_
  35.2 0.0 collective-permute-done.2.refs_2_
  35.2 0.0 copy-done
  35.2 7.1 %feed_forward.1 = bf16[64,8,1024]{2,1,0:T(8,128)(2,1)S(1)} custom-call(bf16[64,8,1024]{2,1,0:T(8,128)(2,1)S(1)} %all_to_all.10.pieces, bf16[64,128]{1,0:T(8,128)(2,1)S(1)} %bitcast.3, bf16[224,8192]{1,0:T(8,128)(2,1)S(1)} %collective-permute-done.refs_0_, bf16[224,8192]{1,0:T(8,128)(2,1)S(1)} %collective-permute-done.1.refs_1_, ...), custom_call_target="tpu_custom_call" | custom-call | flops 1409286144 | bytes 22020096 | tf_op jit(solution)/shard_map/feed_forward/pallas_call | solution.py:270
  42.3 23.0 %all_to_all.11 = bf16[64,8,1024]{2,1,0:T(8,128)(2,1)S(1)} all-to-all(bf16[64,8,1024]{2,1,0:T(8,128)(2,1)S(1)} %feed_forward.1), channel_id=1, replica_groups={{0,42,21,63,34,13,55,26,5,47,18,60,39,10,52,31,2,44,23,57,36,15,49,28,7..., dimensions={0} | all-to-all | bytes 2097152 | tf_op jit(solution)/shard_map/all_to_all | solution.py:345
  65.3 0.2 convert_reduce_fusion
  65.5 0.6 add_convert_fusion
Async XLA Ops:
  0.0 35.2 %collective-permute-start = (bf16[224,8192]{1,0:T(8,128)(2,1)}, bf16[224,8192]{1,0:T(8,128)(2,1)S(1)}, u32[]{:S(2)}, u32[]{:S(2)}) collective-permute-start(bf16[224,8192]{1,0:T(8,128)(2,1)} %bitcast.4), channel_id=1, source_target_pairs={{0,64},{64,0},{1,65},{65,1},{2,66},{66,2},{3,67},{67,3},{4,68},{68... | collective-permute-start | bytes 11010056 | tf_op jit(solution)/shard_map/ppermute | solution.py:329
  0.0 35.2 %copy-start = (bf16[8192]{0:T(1024)(128)(2,1)S(1)}, bf16[8192]{0:T(1024)(128)(2,1)}, u32[]{:S(2)}) copy-start(bf16[8192]{0:T(1024)(128)(2,1)} %param.18) | copy-start | bytes 49156
  0.0 35.2 %collective-permute-start.1 = (bf16[224,8192]{1,0:T(8,128)(2,1)}, bf16[224,8192]{1,0:T(8,128)(2,1)S(1)}, u32[]{:S(2)}, u32[]{:S(2)}) collective-permute-start(bf16[224,8192]{1,0:T(8,128)(2,1)} %bitcast.6), channel_id=1, source_target_pairs={{0,64},{64,0},{1,65},{65,1},{2,66},{66,2},{3,67},{67,3},{4,68},{68... | collective-permute-start | bytes 11010056 | tf_op jit(solution)/shard_map/ppermute | solution.py:329
  0.5 34.7 %collective-permute-start.2 = (bf16[224,8192]{1,0:T(8,128)(2,1)}, bf16[224,8192]{1,0:T(8,128)(2,1)S(1)}, u32[]{:S(2)}, u32[]{:S(2)}) collective-permute-start(bf16[224,8192]{1,0:T(8,128)(2,1)} %refs_5_.1), channel_id=1, source_target_pairs={{0,64},{64,0},{1,65},{65,1},{2,66},{66,2},{3,67},{67,3},{4,68},{68... | collective-permute-start | bytes 11010056 | tf_op jit(solution)/shard_map/ppermute | solution.py:329

commit v4 on v3

--- a/solution.py
+++ b/solution.py
@@ -204,6 +204,11 @@
     out, normed, own_down, sems = refs[6:]
     rows, width = pieces.shape[1:]
     units, features = own_gate.shape
+    role = lax.axis_index("role")
+
+    def slot(chip):
+        return place[chip] + role * (len(place) - 1 - 2 * place[chip])
+
     arrivals = []
     for i, start in enumerate(range(0, features, STEP)):
         span = pl.ds(start, STEP)
@@ -219,7 +224,7 @@
         for half in range(2):
             total = jnp.zeros((rows, width), F32)
             for t in range(tensor):
-                part = pieces[place[(pair * 2 + half) * tensor + t]].astype(F32)
+                part = pieces[slot((pair * 2 + half) * tensor + t)].astype(F32)
                 total = total + part * part
             mean_square = jnp.sum(total, axis=-1, keepdims=True) * (1.0 / features)
             inverse.append(lax.rsqrt(mean_square + 1e-05))
@@ -229,7 +234,7 @@
                 axis=1,
             )
             parts = [
-                pieces[place[(pair * 2 + half) * tensor + t]].astype(F32) * inverse[half] * scale
+                pieces[slot((pair * 2 + half) * tensor + t)].astype(F32) * inverse[half] * scale
                 for half in range(2)
             ]
             normed[pair * 2 * rows : (pair + 1) * 2 * rows, t * width : (t + 1) * width] = (
@@ -248,17 +253,19 @@
         gate, up = sums
         return (gate / (1.0 + jnp.exp(-gate)) * up).astype(BF16).T
 
-    active_own = project((own_gate, own_up))
-    active_mate = project(mate[:2])
+    active = jnp.concatenate([project((own_gate, own_up)), project(mate[:2])], axis=1)
     for one, start in zip(arrivals, range(0, features, STEP)):
         span = slice(start, start + STEP)
-        partial = jnp.dot(active_mate, mate[2][:, span], preferred_element_type=F32)
         one.wait()
-        partial += jnp.dot(active_own, own_down[:, span], preferred_element_type=F32)
+        partial = jnp.dot(
+            active,
+            jnp.concatenate([own_down[:, span], mate[2][:, span]], axis=0),
+            preferred_element_type=F32,
+        )
         for i in range(STEP // width):
             t = start // width + i
             for b in range(batch):
-                out[place[b * tensor + t]] = partial[
+                out[slot(b * tensor + t)] = partial[
                     b * rows : (b + 1) * rows, i * width : (i + 1) * width
                 ].astype(BF16)
 
@@ -288,12 +295,13 @@
 
 
 def chip_order(batch, tensor):
-    side = round((batch * tensor) ** (1 / 3))
+    chips = batch * tensor
+    side = round(chips ** (1 / 3))
+    half = side // 2
     order = []
-    for step in range(batch * tensor):
-        at = 21 * step % (batch * tensor)
-        x, y, z = at % side, at // side % side, at // (side * side)
-        half = side // 2
+    for step in range(chips):
+        at = 21 * step % chips
+        z, y, x = at % side, at // side % side, at // (side * side)
         order.append((y % half * side + x) * tensor + z * half + y // half)
     return order
 
@@ -316,7 +324,7 @@
     chips = batch * tensor
     order = chip_order(batch, tensor)
     place = [order.index(chip) for chip in range(chips)]
-    groups = [[role * chips + chip for chip in order] for role in range(2)]
+    groups = [order, [chips + chip for chip in reversed(order)]]
     exchange = functools.partial(
         lax.all_to_all,
         axis_name=AXES,

time: 66.3 us -> 62.7 us (0.946)
  blocking collectives: 51 us -> 48 us
  Pallas kernels: 13.8 us -> 13.1 us
    all_to_all x1, blocking collectives: 27.9 us -> 25.9 us  [local(): pieces = exchange(copies)]
    all_to_all x1, blocking collectives: 23 us -> 22 us  [local(): received = exchange(partial_out)]
where the time goes in v4:
time: 62.7 us; the launch traced here: 62.4 us
  blocking collectives  48 us (77%)
  Pallas kernels  13.1 us (21%)
  other arithmetic  0.78 us (1%)
    all_to_all x1, blocking collectives, local(): pieces = exchange(copies)  25.9 us
    all_to_all x1, blocking collectives, local(): received = exchange(partial_out)  22 us
    pallas_call x1, Pallas kernels, feed_forward(): pl.pallas_call(functools.partial(feed_forward_kernel, batch, tensor, plac...  6.97 us
    pallas_call x1, Pallas kernels, attention(): pl.pallas_call(attention_kernel, out_shape=(jax.ShapeDtypeStruct((rows, w...  6.13 us
  transfers between devices with their start and end apart: 3, of which 0 were waited for; matrix products, arithmetic and copies ran while one was open for 0% of the time, Pallas kernels for 10%

profile of v4, /device:TPU:0, one launch (start us, length us, event | category | flops | bytes accessed | tf_op | source)
XLA Modules:
  0.0 62.4 jit_solution(7501562776051012954)
XLA Ops:
  0.0 0.0 collective-permute-start
  0.0 0.0 copy-start
  0.0 0.5 collective-permute-start.1
  0.5 0.0 collective-permute-start.2
  0.5 6.1 %attention.1 = (bf16[8,1024]{1,0:T(8,128)(2,1)S(1)}, bf16[64,8,1024]{2,1,0:T(8,128)(2,1)S(1)}, bf16[224,8192]{1,0:T(8,128)(2,1)S(1)}, bf16[224,8192]{1,0:T(8,128)(2,1)S(1)}) custom-call(s32[8]{0:T(128)} %lengths_hbm.1, bf16[8,1024]{1,0:T(8,128)(2,1)} %queries_hbm.1, bf16[8,128]{1,0:T(8,128)(2,1)} %new_keys_hbm.1, bf16[8,128]{1,0:T(8,128)(2,1)} %new_values_hbm.1, ...), custom_call_target="tpu_custom_call" | custom-call | flops 100663296 | bytes 12582912 | tf_op jit(solution)/shard_map/attention/pallas_call | solution.py:167
  6.7 25.9 %all_to_all.10.pieces = bf16[64,8,1024]{2,1,0:T(8,128)(2,1)S(1)} all-to-all(bf16[64,8,1024]{2,1,0:T(8,128)(2,1)S(1)} %get-tuple-element.10), channel_id=1, replica_groups={{0,42,21,63,40,19,61,14,17,59,12,54,57,10,52,31,8,50,29,39,48,27,37,22,..., dimensions={0} | all-to-all | bytes 2097152 | tf_op jit(solution)/shard_map/all_to_all | solution.py:350
  32.6 0.0 collective-permute-done.refs_0_
  32.6 0.0 collective-permute-done.1.refs_1_
  32.6 0.0 collective-permute-done.2.refs_2_
  32.6 0.0 copy-done
  32.6 7.0 %feed_forward.1 = bf16[64,8,1024]{2,1,0:T(8,128)(2,1)S(1)} custom-call(bf16[64,8,1024]{2,1,0:T(8,128)(2,1)S(1)} %all_to_all.10.pieces, bf16[64,128]{1,0:T(8,128)(2,1)S(1)} %bitcast.3, bf16[224,8192]{1,0:T(8,128)(2,1)S(1)} %collective-permute-done.refs_0_, bf16[224,8192]{1,0:T(8,128)(2,1)S(1)} %collective-permute-done.1.refs_1_, ...), custom_call_target="tpu_custom_call" | custom-call | flops 1409286144 | bytes 22020096 | tf_op jit(solution)/shard_map/feed_forward/pallas_call | solution.py:277
  39.6 22.0 %all_to_all.11 = bf16[64,8,1024]{2,1,0:T(8,128)(2,1)S(1)} all-to-all(bf16[64,8,1024]{2,1,0:T(8,128)(2,1)S(1)} %feed_forward.1), channel_id=1, replica_groups={{0,42,21,63,40,19,61,14,17,59,12,54,57,10,52,31,8,50,29,39,48,27,37,22,..., dimensions={0} | all-to-all | bytes 2097152 | tf_op jit(solution)/shard_map/all_to_all | solution.py:353
  61.6 0.2 convert_reduce_fusion
  61.8 0.6 add_convert_fusion
Async XLA Ops:
  0.0 32.6 %collective-permute-start = (bf16[224,8192]{1,0:T(8,128)(2,1)}, bf16[224,8192]{1,0:T(8,128)(2,1)S(1)}, u32[]{:S(2)}, u32[]{:S(2)}) collective-permute-start(bf16[224,8192]{1,0:T(8,128)(2,1)} %bitcast.4), channel_id=1, source_target_pairs={{0,64},{64,0},{1,65},{65,1},{2,66},{66,2},{3,67},{67,3},{4,68},{68... | collective-permute-start | bytes 11010056 | tf_op jit(solution)/shard_map/ppermute | solution.py:337
  0.0 32.6 %copy-start = (bf16[8192]{0:T(1024)(128)(2,1)S(1)}, bf16[8192]{0:T(1024)(128)(2,1)}, u32[]{:S(2)}) copy-start(bf16[8192]{0:T(1024)(128)(2,1)} %param.18) | copy-start | bytes 49156
  0.0 32.6 %collective-permute-start.1 = (bf16[224,8192]{1,0:T(8,128)(2,1)}, bf16[224,8192]{1,0:T(8,128)(2,1)S(1)}, u32[]{:S(2)}, u32[]{:S(2)}) collective-permute-start(bf16[224,8192]{1,0:T(8,128)(2,1)} %bitcast.6), channel_id=1, source_target_pairs={{0,64},{64,0},{1,65},{65,1},{2,66},{66,2},{3,67},{67,3},{4,68},{68... | collective-permute-start | bytes 11010056 | tf_op jit(solution)/shard_map/ppermute | solution.py:337
  0.5 32.1 %collective-permute-start.2 = (bf16[224,8192]{1,0:T(8,128)(2,1)}, bf16[224,8192]{1,0:T(8,128)(2,1)S(1)}, u32[]{:S(2)}, u32[]{:S(2)}) collective-permute-start(bf16[224,8192]{1,0:T(8,128)(2,1)} %refs_5_.1), channel_id=1, source_target_pairs={{0,64},{64,0},{1,65},{65,1},{2,66},{66,2},{3,67},{67,3},{4,68},{68... | collective-permute-start | bytes 11010056 | tf_op jit(solution)/shard_map/ppermute | solution.py:337

commit v5 on v4

--- a/solution.py
+++ b/solution.py
@@ -201,7 +201,7 @@
 
 def feed_forward_kernel(batch, tensor, place, pieces, gain, *refs):
     mate, (own_gate, own_up, down_hbm) = refs[:3], refs[3:6]
-    out, normed, own_down, sems = refs[6:]
+    out, own_down, turned, sems = refs[6:]
     rows, width = pieces.shape[1:]
     units, features = own_gate.shape
     role = lax.axis_index("role")
@@ -219,37 +219,32 @@
     lanes = gain.shape[1]
     tiles = width // lanes
 
-    for pair in range(batch // 2):
-        inverse = []
-        for half in range(2):
-            total = jnp.zeros((rows, width), F32)
-            for t in range(tensor):
-                part = pieces[slot((pair * 2 + half) * tensor + t)].astype(F32)
-                total = total + part * part
-            mean_square = jnp.sum(total, axis=-1, keepdims=True) * (1.0 / features)
-            inverse.append(lax.rsqrt(mean_square + 1e-05))
+    inverse = []
+    for b in range(batch):
+        total = jnp.zeros((rows, width), F32)
         for t in range(tensor):
-            scale = jnp.concatenate(
-                [gain[t * tiles + i : t * tiles + i + 1, :].astype(F32) for i in range(tiles)],
-                axis=1,
-            )
-            parts = [
-                pieces[slot((pair * 2 + half) * tensor + t)].astype(F32) * inverse[half] * scale
-                for half in range(2)
-            ]
-            normed[pair * 2 * rows : (pair + 1) * 2 * rows, t * width : (t + 1) * width] = (
-                jnp.concatenate(parts, axis=0).astype(BF16)
-            )
+            part = pieces[slot(b * tensor + t)].astype(F32)
+            total = total + part * part
+        mean_square = jnp.sum(total, axis=-1, keepdims=True) * (1.0 / features)
+        inverse.append(lax.rsqrt(mean_square + 1e-05))
+    for t in range(tensor):
+        scale = jnp.concatenate(
+            [gain[t * tiles + i : t * tiles + i + 1, :].astype(F32) for i in range(tiles)],
+            axis=1,
+        )
+        parts = [
+            pieces[slot(b * tensor + t)].astype(F32) * inverse[b] * scale for b in range(batch)
+        ]
+        normed = jnp.concatenate(parts, axis=0).astype(BF16)
+        turned[t * width : (t + 1) * width, :] = normed.T
 
     def project(weights):
         sums = [jnp.zeros((units, batch * rows), F32) for _ in range(2)]
         for start in range(0, features, STEP):
             span = slice(start, start + STEP)
-            block = normed[:, span]
+            block = turned[span, :]
             for i in range(2):
-                sums[i] += lax.dot_general(
-                    weights[i][:, span], block, CONTRACT_LAST, preferred_element_type=F32
-                )
+                sums[i] += jnp.dot(weights[i][:, span], block, preferred_element_type=F32)
         gate, up = sums
         return (gate / (1.0 + jnp.exp(-gate)) * up).astype(BF16).T
 
@@ -280,8 +275,8 @@
         in_specs=[VMEM] * 7 + [HBM],
         out_specs=VMEM,
         scratch_shapes=[
-            pltpu.VMEM((batch * rows, features), BF16),
             pltpu.VMEM((units, features), BF16),
+            pltpu.VMEM((features, batch * rows), BF16),
             pltpu.SemaphoreType.DMA((features // STEP,)),
         ],
         compiler_params=pltpu.CompilerParams(vmem_limit_bytes=16 << 20),

time: 62.7 us -> 61.7 us (0.984)
  Pallas kernels: 13.1 us -> 11.9 us
    pallas_call x1, Pallas kernels: 6.97 us -> 5.98 us  [feed_forward(): pl.pallas_call(functools.partial(feed_forward_kernel, batch, tensor, plac...]
where the time goes in v5:
time: 61.7 us; the launch traced here: 61.5 us
  blocking collectives  48.2 us (78%)
  Pallas kernels  11.9 us (19%)
  other arithmetic  0.78 us (1%)
    all_to_all x1, blocking collectives, local(): pieces = exchange(copies)  26.1 us
    all_to_all x1, blocking collectives, local(): received = exchange(partial_out)  22.1 us
    pallas_call x1, Pallas kernels, feed_forward(): pl.pallas_call(functools.partial(feed_forward_kernel, batch, tensor, plac...  5.98 us
    pallas_call x1, Pallas kernels, attention(): pl.pallas_call(attention_kernel, out_shape=(jax.ShapeDtypeStruct((rows, w...  5.97 us
  transfers between devices with their start and end apart: 3, of which 0 were waited for; matrix products, arithmetic and copies ran while one was open for 0% of the time, Pallas kernels for 10%

profile of v5, /device:TPU:0, one launch (start us, length us, event | category | flops | bytes accessed | tf_op | source)
XLA Modules:
  0.0 61.5 jit_solution(7083696100322702475)
XLA Ops:
  0.0 0.0 collective-permute-start
  0.0 0.0 copy-start
  0.0 0.5 collective-permute-start.1
  0.5 0.0 collective-permute-start.2
  0.5 6.0 %attention.1 = (bf16[8,1024]{1,0:T(8,128)(2,1)S(1)}, bf16[64,8,1024]{2,1,0:T(8,128)(2,1)S(1)}, bf16[224,8192]{1,0:T(8,128)(2,1)S(1)}, bf16[224,8192]{1,0:T(8,128)(2,1)S(1)}) custom-call(s32[8]{0:T(128)} %lengths_hbm.1, bf16[8,1024]{1,0:T(8,128)(2,1)} %queries_hbm.1, bf16[8,128]{1,0:T(8,128)(2,1)} %new_keys_hbm.1, bf16[8,128]{1,0:T(8,128)(2,1)} %new_values_hbm.1, ...), custom_call_target="tpu_custom_call" | custom-call | flops 100663296 | bytes 12582912 | tf_op jit(solution)/shard_map/attention/pallas_call | solution.py:167
  6.5 26.1 %all_to_all.10.pieces = bf16[64,8,1024]{2,1,0:T(8,128)(2,1)S(1)} all-to-all(bf16[64,8,1024]{2,1,0:T(8,128)(2,1)S(1)} %get-tuple-element.10), channel_id=1, replica_groups={{0,42,21,63,40,19,61,14,17,59,12,54,57,10,52,31,8,50,29,39,48,27,37,22,..., dimensions={0} | all-to-all | bytes 2097152 | tf_op jit(solution)/shard_map/all_to_all | solution.py:345
  32.6 0.0 collective-permute-done.refs_0_
  32.6 0.0 collective-permute-done.1.refs_1_
  32.6 0.0 collective-permute-done.2.refs_2_
  32.6 0.0 copy-done
  32.6 6.0 %feed_forward.1 = bf16[64,8,1024]{2,1,0:T(8,128)(2,1)S(1)} custom-call(bf16[64,8,1024]{2,1,0:T(8,128)(2,1)S(1)} %all_to_all.10.pieces, bf16[64,128]{1,0:T(8,128)(2,1)S(1)} %bitcast.3, bf16[224,8192]{1,0:T(8,128)(2,1)S(1)} %collective-permute-done.refs_0_, bf16[224,8192]{1,0:T(8,128)(2,1)S(1)} %collective-permute-done.1.refs_1_, ...), custom_call_target="tpu_custom_call" | custom-call | flops 1409286144 | bytes 22020096 | tf_op jit(solution)/shard_map/feed_forward/pallas_call | solution.py:272
  38.6 22.1 %all_to_all.11 = bf16[64,8,1024]{2,1,0:T(8,128)(2,1)S(1)} all-to-all(bf16[64,8,1024]{2,1,0:T(8,128)(2,1)S(1)} %feed_forward.1), channel_id=1, replica_groups={{0,42,21,63,40,19,61,14,17,59,12,54,57,10,52,31,8,50,29,39,48,27,37,22,..., dimensions={0} | all-to-all | bytes 2097152 | tf_op jit(solution)/shard_map/all_to_all | solution.py:348
  60.7 0.2 convert_reduce_fusion
  60.9 0.6 add_convert_fusion
Async XLA Ops:
  0.0 32.6 %collective-permute-start = (bf16[224,8192]{1,0:T(8,128)(2,1)}, bf16[224,8192]{1,0:T(8,128)(2,1)S(1)}, u32[]{:S(2)}, u32[]{:S(2)}) collective-permute-start(bf16[224,8192]{1,0:T(8,128)(2,1)} %bitcast.4), channel_id=1, source_target_pairs={{0,64},{64,0},{1,65},{65,1},{2,66},{66,2},{3,67},{67,3},{4,68},{68... | collective-permute-start | bytes 11010056 | tf_op jit(solution)/shard_map/ppermute | solution.py:332
  0.0 32.6 %copy-start = (bf16[8192]{0:T(1024)(128)(2,1)S(1)}, bf16[8192]{0:T(1024)(128)(2,1)}, u32[]{:S(2)}) copy-start(bf16[8192]{0:T(1024)(128)(2,1)} %param.18) | copy-start | bytes 49156
  0.0 32.6 %collective-permute-start.1 = (bf16[224,8192]{1,0:T(8,128)(2,1)}, bf16[224,8192]{1,0:T(8,128)(2,1)S(1)}, u32[]{:S(2)}, u32[]{:S(2)}) collective-permute-start(bf16[224,8192]{1,0:T(8,128)(2,1)} %bitcast.6), channel_id=1, source_target_pairs={{0,64},{64,0},{1,65},{65,1},{2,66},{66,2},{3,67},{67,3},{4,68},{68... | collective-permute-start | bytes 11010056 | tf_op jit(solution)/shard_map/ppermute | solution.py:332
  0.5 32.1 %collective-permute-start.2 = (bf16[224,8192]{1,0:T(8,128)(2,1)}, bf16[224,8192]{1,0:T(8,128)(2,1)S(1)}, u32[]{:S(2)}, u32[]{:S(2)}) collective-permute-start(bf16[224,8192]{1,0:T(8,128)(2,1)} %refs_5_.1), channel_id=1, source_target_pairs={{0,64},{64,0},{1,65},{65,1},{2,66},{66,2},{3,67},{67,3},{4,68},{68... | collective-permute-start | bytes 11010056 | tf_op jit(solution)/shard_map/ppermute | solution.py:332

commit v6 on v5

--- a/solution.py
+++ b/solution.py
@@ -10,7 +10,8 @@
 AXES = ("role", "batch", "tensor")
 CHIPS = ("batch", "tensor")
 PACK = 16
-TOGETHER = 4
+TOGETHER = 8
+WHOLE = 3
 STAGE_AFTER = 0
 STEP = 4096
 CONTRACT_LAST = (((1,), (1,)), ((), ()))
@@ -58,8 +59,11 @@
 
     def copy(which, row):
         source, target = ((keys_hbm, keys), (values_hbm, values))[which]
-        length = (lengths[row] + PACK - 1) // PACK * PACK
-        span = pl.ds(0, pl.multiple_of(length, PACK))
+        if which == 0 and row < WHOLE:
+            span = pl.ds(0, cache_len)
+        else:
+            length = (lengths[row] + PACK - 1) // PACK * PACK
+            span = pl.ds(0, pl.multiple_of(length, PACK))
         return pltpu.make_async_copy(
             source.at[row, 0, span], target.at[row, span], sems.at[which, row]
         )
@@ -78,12 +82,15 @@
     ]
     for one in small:
         one.start()
+    for row in range(WHOLE):
+        copy(0, row).start()
     for row in range(rows):
         values[row] = jnp.zeros((cache_len, head), BF16)
     small[0].wait()
     for which in range(2):
         for row in range(rows):
-            copy(which, row).start()
+            if which or row >= WHOLE:
+                copy(which, row).start()
     for one in small[1:]:
         one.wait()
 
@@ -100,13 +107,13 @@
     )
     place = lax.broadcasted_iota(jnp.int32, (group, cache_len), 1)
     own_probs = []
-    for first in range(0, rows, TOGETHER):
-        for row in range(first, first + TOGETHER):
+    for first, last in ((0, WHOLE), (WHOLE, rows)):
+        for row in range(first, last):
             copy(0, row).wait()
         if first == STAGE_AFTER:
             for one in staged:
                 one.start()
-        for row in range(first, first + TOGETHER):
+        for row in range(first, last):
             products = lax.dot_general(
                 heads[row].astype(BF16), keys[row], CONTRACT_LAST, preferred_element_type=F32
             )

time: 61.7 us -> 61.3 us (level)
  transfers between devices with their start and end apart: 3 -> 3, of which waited for: 0 -> 0; matrix products, arithmetic and copies ran while one was open for 0% -> 0% of each run, Pallas kernels for 10% -> 9%
where the time goes in v6:
time: 61.3 us; the launch traced here: 61.1 us
  blocking collectives  48.2 us (79%)
  Pallas kernels  11.5 us (19%)
  other arithmetic  0.78 us (1%)
    all_to_all x1, blocking collectives, local(): pieces = exchange(copies)  26.2 us
    all_to_all x1, blocking collectives, local(): received = exchange(partial_out)  22 us
    pallas_call x1, Pallas kernels, feed_forward(): pl.pallas_call(functools.partial(feed_forward_kernel, batch, tensor, plac...  5.98 us
    pallas_call x1, Pallas kernels, attention(): pl.pallas_call(attention_kernel, out_shape=(jax.ShapeDtypeStruct((rows, w...  5.53 us
  transfers between devices with their start and end apart: 3, of which 0 were waited for; matrix products, arithmetic and copies ran while one was open for 0% of the time, Pallas kernels for 9%

profile of v6, /device:TPU:0, one launch (start us, length us, event | category | flops | bytes accessed | tf_op | source)
XLA Modules:
  0.0 61.1 jit_solution(13116306229380961365)
XLA Ops:
  0.0 0.0 collective-permute-start
  0.0 0.0 copy-start
  0.0 0.5 collective-permute-start.1
  0.5 0.0 collective-permute-start.2
  0.5 5.5 %attention.1 = (bf16[8,1024]{1,0:T(8,128)(2,1)S(1)}, bf16[64,8,1024]{2,1,0:T(8,128)(2,1)S(1)}, bf16[224,8192]{1,0:T(8,128)(2,1)S(1)}, bf16[224,8192]{1,0:T(8,128)(2,1)S(1)}) custom-call(s32[8]{0:T(128)} %lengths_hbm.1, bf16[8,1024]{1,0:T(8,128)(2,1)} %queries_hbm.1, bf16[8,128]{1,0:T(8,128)(2,1)} %new_keys_hbm.1, bf16[8,128]{1,0:T(8,128)(2,1)} %new_values_hbm.1, ...), custom_call_target="tpu_custom_call" | custom-call | flops 100663296 | bytes 12582912 | tf_op jit(solution)/shard_map/attention/pallas_call | solution.py:174
  6.1 26.2 %all_to_all.10.pieces = bf16[64,8,1024]{2,1,0:T(8,128)(2,1)S(1)} all-to-all(bf16[64,8,1024]{2,1,0:T(8,128)(2,1)S(1)} %get-tuple-element.10), channel_id=1, replica_groups={{0,42,21,63,40,19,61,14,17,59,12,54,57,10,52,31,8,50,29,39,48,27,37,22,..., dimensions={0} | all-to-all | bytes 2097152 | tf_op jit(solution)/shard_map/all_to_all | solution.py:352
  32.3 0.0 collective-permute-done.refs_0_
  32.3 0.0 collective-permute-done.1.refs_1_
  32.3 0.0 collective-permute-done.2.refs_2_
  32.3 0.0 copy-done
  32.3 6.0 %feed_forward.1 = bf16[64,8,1024]{2,1,0:T(8,128)(2,1)S(1)} custom-call(bf16[64,8,1024]{2,1,0:T(8,128)(2,1)S(1)} %all_to_all.10.pieces, bf16[64,128]{1,0:T(8,128)(2,1)S(1)} %bitcast.3, bf16[224,8192]{1,0:T(8,128)(2,1)S(1)} %collective-permute-done.refs_0_, bf16[224,8192]{1,0:T(8,128)(2,1)S(1)} %collective-permute-done.1.refs_1_, ...), custom_call_target="tpu_custom_call" | custom-call | flops 1409286144 | bytes 22020096 | tf_op jit(solution)/shard_map/feed_forward/pallas_call | solution.py:279
  38.3 22.0 %all_to_all.11 = bf16[64,8,1024]{2,1,0:T(8,128)(2,1)S(1)} all-to-all(bf16[64,8,1024]{2,1,0:T(8,128)(2,1)S(1)} %feed_forward.1), channel_id=1, replica_groups={{0,42,21,63,40,19,61,14,17,59,12,54,57,10,52,31,8,50,29,39,48,27,37,22,..., dimensions={0} | all-to-all | bytes 2097152 | tf_op jit(solution)/shard_map/all_to_all | solution.py:355
  60.3 0.2 convert_reduce_fusion
  60.5 0.6 %add_convert_fusion = bf16[8,1024]{1,0:T(8,128)(2,1)} fusion(f32[8,1024]{1,0:T(8,128)S(1)} %convert_reduce_fusion, bf16[8,1024]{1,0:T(8,128)(2,1)S(1)} %get-tuple-element.9), kind=kLoop, calls=%fused_computation.1 | loop fusion | flops 24576 | bytes 65536 | tf_op jit(solution)/shard_map/convert_element_type | solution.py:357
Async XLA Ops:
  0.0 32.3 %collective-permute-start = (bf16[224,8192]{1,0:T(8,128)(2,1)}, bf16[224,8192]{1,0:T(8,128)(2,1)S(1)}, u32[]{:S(2)}, u32[]{:S(2)}) collective-permute-start(bf16[224,8192]{1,0:T(8,128)(2,1)} %bitcast.4), channel_id=1, source_target_pairs={{0,64},{64,0},{1,65},{65,1},{2,66},{66,2},{3,67},{67,3},{4,68},{68... | collective-permute-start | bytes 11010056 | tf_op jit(solution)/shard_map/ppermute | solution.py:339
  0.0 32.3 %copy-start = (bf16[8192]{0:T(1024)(128)(2,1)S(1)}, bf16[8192]{0:T(1024)(128)(2,1)}, u32[]{:S(2)}) copy-start(bf16[8192]{0:T(1024)(128)(2,1)} %param.18) | copy-start | bytes 49156
  0.0 32.3 %collective-permute-start.1 = (bf16[224,8192]{1,0:T(8,128)(2,1)}, bf16[224,8192]{1,0:T(8,128)(2,1)S(1)}, u32[]{:S(2)}, u32[]{:S(2)}) collective-permute-start(bf16[224,8192]{1,0:T(8,128)(2,1)} %bitcast.6), channel_id=1, source_target_pairs={{0,64},{64,0},{1,65},{65,1},{2,66},{66,2},{3,67},{67,3},{4,68},{68... | collective-permute-start | bytes 11010056 | tf_op jit(solution)/shard_map/ppermute | solution.py:339
  0.5 31.8 %collective-permute-start.2 = (bf16[224,8192]{1,0:T(8,128)(2,1)}, bf16[224,8192]{1,0:T(8,128)(2,1)S(1)}, u32[]{:S(2)}, u32[]{:S(2)}) collective-permute-start(bf16[224,8192]{1,0:T(8,128)(2,1)} %refs_5_.1), channel_id=1, source_target_pairs={{0,64},{64,0},{1,65},{65,1},{2,66},{66,2},{3,67},{67,3},{4,68},{68... | collective-permute-start | bytes 11010056 | tf_op jit(solution)/shard_map/ppermute | solution.py:339

commit v7 on v6

--- a/solution.py
+++ b/solution.py
@@ -84,13 +84,17 @@
         one.start()
     for row in range(WHOLE):
         copy(0, row).start()
-    for row in range(rows):
+    half = rows // 2
+    for row in range(half):
         values[row] = jnp.zeros((cache_len, head), BF16)
     small[0].wait()
-    for which in range(2):
-        for row in range(rows):
-            if which or row >= WHOLE:
-                copy(which, row).start()
+    for row in range(WHOLE, rows):
+        copy(0, row).start()
+    for row in range(half):
+        copy(1, row).start()
+    for row in range(half, rows):
+        values[row] = jnp.zeros((cache_len, head), BF16)
+        copy(1, row).start()
     for one in small[1:]:
         one.wait()
 
@@ -245,17 +249,20 @@
         normed = jnp.concatenate(parts, axis=0).astype(BF16)
         turned[t * width : (t + 1) * width, :] = normed.T
 
-    def project(weights):
-        sums = [jnp.zeros((units, batch * rows), F32) for _ in range(2)]
-        for start in range(0, features, STEP):
-            span = slice(start, start + STEP)
-            block = turned[span, :]
-            for i in range(2):
-                sums[i] += jnp.dot(weights[i][:, span], block, preferred_element_type=F32)
-        gate, up = sums
-        return (gate / (1.0 + jnp.exp(-gate)) * up).astype(BF16).T
-
-    active = jnp.concatenate([project((own_gate, own_up)), project(mate[:2])], axis=1)
+    projections = (own_gate, own_up, mate[0], mate[1])
+    sums = [jnp.zeros((units, batch * rows), F32) for _ in projections]
+    for start in range(0, features, STEP):
+        span = slice(start, start + STEP)
+        block = turned[span, :]
+        for i, w in enumerate(projections):
+            sums[i] += jnp.dot(w[:, span], block, preferred_element_type=F32)
+    active = jnp.concatenate(
+        [
+            (gate / (1.0 + jnp.exp(-gate)) * up).astype(BF16).T
+            for gate, up in (sums[:2], sums[2:])
+        ],
+        axis=1,
+    )
     for one, start in zip(arrivals, range(0, features, STEP)):
         span = slice(start, start + STEP)
         one.wait()
@@ -353,8 +360,10 @@
     own = (*near, own[2])
     partial_out = feed_forward(pieces, norm_gain, own, mate, batch, tensor, place)
     received = exchange(partial_out)
-    summed = jnp.sum(received.astype(F32), axis=0)
-    return (hidden_state.astype(F32) + summed).astype(BF16)
+    total = hidden_state.astype(F32)
+    for chip in range(chips):
+        total += received[chip].astype(F32)
+    return total.astype(BF16)
 
 
 def solution(mesh):

time: 61.3 us -> 61.3 us (level)
  no operation moved by 1% of the time
where the time goes in v7:
time: 61.3 us; the launch traced here: 61.1 us
  blocking collectives  48 us (78%)
  Pallas kernels  11.8 us (19%)
  other arithmetic  0.79 us (1%)
    all_to_all x1, blocking collectives, local(): pieces = exchange(copies)  26 us
    all_to_all x1, blocking collectives, local(): received = exchange(partial_out)  22 us
    pallas_call x1, Pallas kernels, feed_forward(): pl.pallas_call(functools.partial(feed_forward_kernel, batch, tensor, plac...  5.98 us
    pallas_call x1, Pallas kernels, attention(): pl.pallas_call(attention_kernel, out_shape=(jax.ShapeDtypeStruct((rows, w...  5.8 us
  transfers between devices with their start and end apart: 3, of which 0 were waited for; matrix products, arithmetic and copies ran while one was open for 0% of the time, Pallas kernels for 9%

profile of v7, /device:TPU:0, one launch (start us, length us, event | category | flops | bytes accessed | tf_op | source)
XLA Modules:
  0.0 61.1 jit_solution(13007776804422153893)
XLA Ops:
  0.0 0.0 collective-permute-start
  0.0 0.0 copy-start
  0.0 0.5 collective-permute-start.1
  0.5 0.0 collective-permute-start.2
  0.5 5.8 %attention.1 = (bf16[8,1024]{1,0:T(8,128)(2,1)S(1)}, bf16[64,8,1024]{2,1,0:T(8,128)(2,1)S(1)}, bf16[224,8192]{1,0:T(8,128)(2,1)S(1)}, bf16[224,8192]{1,0:T(8,128)(2,1)S(1)}) custom-call(s32[8]{0:T(128)} %lengths_hbm.1, bf16[8,1024]{1,0:T(8,128)(2,1)} %queries_hbm.1, bf16[8,128]{1,0:T(8,128)(2,1)} %new_keys_hbm.1, bf16[8,128]{1,0:T(8,128)(2,1)} %new_values_hbm.1, ...), custom_call_target="tpu_custom_call" | custom-call | flops 100663296 | bytes 12582912 | tf_op jit(solution)/shard_map/attention/pallas_call | solution.py:178
  6.3 26.0 %all_to_all.10.pieces = bf16[64,8,1024]{2,1,0:T(8,128)(2,1)S(1)} all-to-all(bf16[64,8,1024]{2,1,0:T(8,128)(2,1)S(1)} %get-tuple-element.10), channel_id=1, replica_groups={{0,42,21,63,40,19,61,14,17,59,12,54,57,10,52,31,8,50,29,39,48,27,37,22,..., dimensions={0} | all-to-all | bytes 2097152 | tf_op jit(solution)/shard_map/all_to_all | solution.py:359
  32.3 0.0 collective-permute-done.refs_0_
  32.3 0.0 collective-permute-done.1.refs_1_
  32.3 0.0 collective-permute-done.2.refs_2_
  32.3 0.0 copy-done
  32.3 6.0 %feed_forward.1 = bf16[64,8,1024]{2,1,0:T(8,128)(2,1)S(1)} custom-call(bf16[64,8,1024]{2,1,0:T(8,128)(2,1)S(1)} %all_to_all.10.pieces, bf16[64,128]{1,0:T(8,128)(2,1)S(1)} %bitcast.323, bf16[224,8192]{1,0:T(8,128)(2,1)S(1)} %collective-permute-done.refs_0_, bf16[224,8192]{1,0:T(8,128)(2,1)S(1)} %collective-permute-done.1.refs_1_, ...), custom_call_target="tpu_custom_call" | custom-call | flops 1409286144 | bytes 22020096 | tf_op jit(solution)/shard_map/feed_forward/pallas_call | solution.py:286
  38.3 22.0 %all_to_all.11 = bf16[64,8,1024]{2,1,0:T(8,128)(2,1)S(1)} all-to-all(bf16[64,8,1024]{2,1,0:T(8,128)(2,1)S(1)} %feed_forward.1), channel_id=1, replica_groups={{0,42,21,63,40,19,61,14,17,59,12,54,57,10,52,31,8,50,29,39,48,27,37,22,..., dimensions={0} | all-to-all | bytes 2097152 | tf_op jit(solution)/shard_map/all_to_all | solution.py:362
  60.3 0.8 %fusion = bf16[8,1024]{1,0:T(8,128)(2,1)} fusion(bf16[8,1024]{1,0:T(8,128)(2,1)S(1)} %get-tuple-element.9, bf16[64,8,1024]{2,1,0:T(8,128)(2,1)S(1)} %all_to_all.11), kind=kLoop, calls=%fused_computation.1 | loop fusion | flops 1064960 | bytes 1081344 | tf_op jit(solution)/shard_map/convert_element_type | solution.py:366
Async XLA Ops:
  0.0 32.3 %collective-permute-start = (bf16[224,8192]{1,0:T(8,128)(2,1)}, bf16[224,8192]{1,0:T(8,128)(2,1)S(1)}, u32[]{:S(2)}, u32[]{:S(2)}) collective-permute-start(bf16[224,8192]{1,0:T(8,128)(2,1)} %bitcast.324), channel_id=1, source_target_pairs={{0,64},{64,0},{1,65},{65,1},{2,66},{66,2},{3,67},{67,3},{4,68},{68... | collective-permute-start | bytes 11010056 | tf_op jit(solution)/shard_map/ppermute | solution.py:346
  0.0 32.3 %copy-start = (bf16[8192]{0:T(1024)(128)(2,1)S(1)}, bf16[8192]{0:T(1024)(128)(2,1)}, u32[]{:S(2)}) copy-start(bf16[8192]{0:T(1024)(128)(2,1)} %param.18) | copy-start | bytes 49156
  0.0 32.3 %collective-permute-start.1 = (bf16[224,8192]{1,0:T(8,128)(2,1)}, bf16[224,8192]{1,0:T(8,128)(2,1)S(1)}, u32[]{:S(2)}, u32[]{:S(2)}) collective-permute-start(bf16[224,8192]{1,0:T(8,128)(2,1)} %bitcast.326), channel_id=1, source_target_pairs={{0,64},{64,0},{1,65},{65,1},{2,66},{66,2},{3,67},{67,3},{4,68},{68... | collective-permute-start | bytes 11010056 | tf_op jit(solution)/shard_map/ppermute | solution.py:346
  0.5 31.8 %collective-permute-start.2 = (bf16[224,8192]{1,0:T(8,128)(2,1)}, bf16[224,8192]{1,0:T(8,128)(2,1)S(1)}, u32[]{:S(2)}, u32[]{:S(2)}) collective-permute-start(bf16[224,8192]{1,0:T(8,128)(2,1)} %refs_5_.1), channel_id=1, source_target_pairs={{0,64},{64,0},{1,65},{65,1},{2,66},{66,2},{3,67},{67,3},{4,68},{68... | collective-permute-start | bytes 11010056 | tf_op jit(solution)/shard_map/ppermute | solution.py:346

commit v8 on v7

--- a/solution.py
+++ b/solution.py
@@ -310,7 +310,7 @@
     order = []
     for step in range(chips):
         at = 21 * step % chips
-        z, y, x = at % side, at // side % side, at // (side * side)
+        y, z, x = at % side, at // side % side, at // (side * side)
         order.append((y % half * side + x) * tensor + z * half + y // half)
     return order
 

time: 61.3 us -> 61.3 us (level)
  no operation moved by 1% of the time
where the time goes in v8:
time: 61.3 us; the launch traced here: 61.2 us
  blocking collectives  48.4 us (79%)
  Pallas kernels  11.4 us (19%)
  other arithmetic  0.79 us (1%)
    all_to_all x1, blocking collectives, local(): pieces = exchange(copies)  26.4 us
    all_to_all x1, blocking collectives, local(): received = exchange(partial_out)  21.9 us
    pallas_call x1, Pallas kernels, feed_forward(): pl.pallas_call(functools.partial(feed_forward_kernel, batch, tensor, plac...  5.99 us
    pallas_call x1, Pallas kernels, attention(): pl.pallas_call(attention_kernel, out_shape=(jax.ShapeDtypeStruct((rows, w...  5.46 us
  transfers between devices with their start and end apart: 3, of which 0 were waited for; matrix products, arithmetic and copies ran while one was open for 0% of the time, Pallas kernels for 9%

profile of v8, /device:TPU:0, one launch (start us, length us, event | category | flops | bytes accessed | tf_op | source)
XLA Modules:
  0.0 61.2 jit_solution(11284247053914939136)
XLA Ops:
  0.0 0.0 collective-permute-start
  0.0 0.0 copy-start
  0.0 0.5 collective-permute-start.1
  0.5 0.0 collective-permute-start.2
  0.5 5.5 %attention.1 = (bf16[8,1024]{1,0:T(8,128)(2,1)S(1)}, bf16[64,8,1024]{2,1,0:T(8,128)(2,1)S(1)}, bf16[224,8192]{1,0:T(8,128)(2,1)S(1)}, bf16[224,8192]{1,0:T(8,128)(2,1)S(1)}) custom-call(s32[8]{0:T(128)} %lengths_hbm.1, bf16[8,1024]{1,0:T(8,128)(2,1)} %queries_hbm.1, bf16[8,128]{1,0:T(8,128)(2,1)} %new_keys_hbm.1, bf16[8,128]{1,0:T(8,128)(2,1)} %new_values_hbm.1, ...), custom_call_target="tpu_custom_call" | custom-call | flops 100663296 | bytes 12582912 | tf_op jit(solution)/shard_map/attention/pallas_call | solution.py:178
  6.0 26.4 %all_to_all.10.pieces = bf16[64,8,1024]{2,1,0:T(8,128)(2,1)S(1)} all-to-all(bf16[64,8,1024]{2,1,0:T(8,128)(2,1)S(1)} %get-tuple-element.10), channel_id=1, replica_groups={{0,42,21,63,10,52,31,41,20,62,9,51,30,40,19,61,8,50,29,39,18,60,7,49,28..., dimensions={0} | all-to-all | bytes 2097152 | tf_op jit(solution)/shard_map/all_to_all | solution.py:359
  32.4 0.0 collective-permute-done.refs_0_
  32.4 0.0 collective-permute-done.1.refs_1_
  32.4 0.0 collective-permute-done.2.refs_2_
  32.4 0.0 copy-done
  32.4 6.0 %feed_forward.1 = bf16[64,8,1024]{2,1,0:T(8,128)(2,1)S(1)} custom-call(bf16[64,8,1024]{2,1,0:T(8,128)(2,1)S(1)} %all_to_all.10.pieces, bf16[64,128]{1,0:T(8,128)(2,1)S(1)} %bitcast.323, bf16[224,8192]{1,0:T(8,128)(2,1)S(1)} %collective-permute-done.refs_0_, bf16[224,8192]{1,0:T(8,128)(2,1)S(1)} %collective-permute-done.1.refs_1_, ...), custom_call_target="tpu_custom_call" | custom-call | flops 1409286144 | bytes 22020096 | tf_op jit(solution)/shard_map/feed_forward/pallas_call | solution.py:286
  38.4 21.9 %all_to_all.11 = bf16[64,8,1024]{2,1,0:T(8,128)(2,1)S(1)} all-to-all(bf16[64,8,1024]{2,1,0:T(8,128)(2,1)S(1)} %feed_forward.1), channel_id=1, replica_groups={{0,42,21,63,10,52,31,41,20,62,9,51,30,40,19,61,8,50,29,39,18,60,7,49,28..., dimensions={0} | all-to-all | bytes 2097152 | tf_op jit(solution)/shard_map/all_to_all | solution.py:362
  60.4 0.8 %fusion = bf16[8,1024]{1,0:T(8,128)(2,1)} fusion(bf16[8,1024]{1,0:T(8,128)(2,1)S(1)} %get-tuple-element.9, bf16[64,8,1024]{2,1,0:T(8,128)(2,1)S(1)} %all_to_all.11), kind=kLoop, calls=%fused_computation.1 | loop fusion | flops 1064960 | bytes 1081344 | tf_op jit(solution)/shard_map/convert_element_type | solution.py:366
Async XLA Ops:
  0.0 32.4 %collective-permute-start = (bf16[224,8192]{1,0:T(8,128)(2,1)}, bf16[224,8192]{1,0:T(8,128)(2,1)S(1)}, u32[]{:S(2)}, u32[]{:S(2)}) collective-permute-start(bf16[224,8192]{1,0:T(8,128)(2,1)} %bitcast.324), channel_id=1, source_target_pairs={{0,64},{64,0},{1,65},{65,1},{2,66},{66,2},{3,67},{67,3},{4,68},{68... | collective-permute-start | bytes 11010056 | tf_op jit(solution)/shard_map/ppermute | solution.py:346
  0.0 32.4 %copy-start = (bf16[8192]{0:T(1024)(128)(2,1)S(1)}, bf16[8192]{0:T(1024)(128)(2,1)}, u32[]{:S(2)}) copy-start(bf16[8192]{0:T(1024)(128)(2,1)} %param.18) | copy-start | bytes 49156
  0.0 32.4 %collective-permute-start.1 = (bf16[224,8192]{1,0:T(8,128)(2,1)}, bf16[224,8192]{1,0:T(8,128)(2,1)S(1)}, u32[]{:S(2)}, u32[]{:S(2)}) collective-permute-start(bf16[224,8192]{1,0:T(8,128)(2,1)} %bitcast.326), channel_id=1, source_target_pairs={{0,64},{64,0},{1,65},{65,1},{2,66},{66,2},{3,67},{67,3},{4,68},{68... | collective-permute-start | bytes 11010056 | tf_op jit(solution)/shard_map/ppermute | solution.py:346
  0.5 31.9 %collective-permute-start.2 = (bf16[224,8192]{1,0:T(8,128)(2,1)}, bf16[224,8192]{1,0:T(8,128)(2,1)S(1)}, u32[]{:S(2)}, u32[]{:S(2)}) collective-permute-start(bf16[224,8192]{1,0:T(8,128)(2,1)} %refs_5_.1), channel_id=1, source_target_pairs={{0,64},{64,0},{1,65},{65,1},{2,66},{66,2},{3,67},{67,3},{4,68},{68... | collective-permute-start | bytes 11010056 | tf_op jit(solution)/shard_map/ppermute | solution.py:346
